TPU v7x, 512 devices: a whole 4x8x8 slice. The times are simulated.
512 devices in a mesh: morton: 64 (over z, y), slab: 8 (over x, core).
Axes of the slice: x: 4, y: 8, z: 8, core: 2. Of those that a mesh axis runs over, the one named last changes fastest.
Arguments:
- sources: bfloat16 [1024, 32, 256], P('morton', None, 'slab'), may hold values from -6 to 6
- basis_in: bfloat16 [1024, 64, 256], P('morton', None, 'slab'), may hold values from -0.375 to 0.375
- basis_out: bfloat16 [1024, 64, 256], P('morton', None, 'slab'), may hold values from -0.75 to 0.75
- transfer: float32 [1920, 64, 64], P('morton'), may hold values from -0.5 to 0.5
- coupling: float32 [1984, 16, 64, 64], P('morton', 'slab'), may hold values from -0.1875 to 0.1875
- coupling_list: int32 [1984, 16], P('morton', 'slab'), may hold values from 0 to 1983, as said below
- near_block: bfloat16 [12288, 256, 256], P('morton', 'slab'), may hold values from -0.15625 to 0.15625
- near_scale: float32 [12288], P('morton'), may hold values from 0.25 to 4
- near_target: int32 [12288], P('morton'), may hold values from 0 to 1023, as said below
- near_source: int32 [12288], P('morton'), may hold values from 0 to 1023, as said below
- near_count: int32 [64], P('morton'), may hold values from 48 to 192
Outputs:
- product: float32 [1024, 32, 256], P('morton', None, 'slab')
Inputs may be any that keep to these rules, and one draw needn't show every extreme that they name: `coupling_list`: an entry of the list of a cluster below the top names a different cluster of the same level owned by the same index of morton or by either Morton neighbour; an entry of a top cluster's list names the top cluster of another index of morton. `near_target`: the slots of index m of morton name leaves of index m; the first 16 slots of every index name its leaves in order. `near_source`: the slots of index m of morton name leaves owned by m, m - 1 or m + 1; the first 16 slots of every index name the same leaf as near_target.
All inputs are finite; a program needn't handle non-finite values.
Results may differ from a plain program's by a relative error of at most 0.0021.
Values may be sent and summed in bfloat16 or wider, within the bound.
No kernel may reach another device: no remote copies, remote signals or barrier semaphores. Data moves between devices by JAX's collectives and lax.ppermute only.
A program may use at most 64 MiB of HBM per device.

v0:
```python
import jax
import jax.numpy as jnp
from jax import lax
from jax.sharding import PartitionSpec as P


def extended(array, sides, width):
    for axis, dim in sides:
        count, length = (lax.axis_size(axis), array.shape[dim])
        up = [(i, (i + 1) % count) for i in range(count - 1)]
        down = [(j, i) for i, j in up]
        last = lax.slice_in_dim(array, length - width, length, axis=dim)
        leading = lax.slice_in_dim(array, 0, width, axis=dim)
        before = lax.ppermute(last, axis, up)
        after = lax.ppermute(leading, axis, down)
        array = jnp.concatenate([before, array, after], axis=dim)
    return array


def level_sizes(leaves):
    return [leaves >> height for height in range(leaves.bit_length())]


def upward(leaf_skeleton, transfer):
    gathered_levels = [leaf_skeleton]
    current = leaf_skeleton
    offset = 0
    for cluster_count in level_sizes(leaf_skeleton.shape[0])[:-1]:
        matrices = transfer[offset : offset + cluster_count]
        carried = jnp.einsum("cij,cjr->cir", matrices, current, precision=lax.Precision.HIGHEST)
        current = carried.reshape(cluster_count // 2, 2, carried.shape[1], carried.shape[2]).sum(
            axis=1
        )
        gathered_levels.append(current)
        offset = offset + cluster_count
    return jnp.concatenate(gathered_levels, axis=0)


def downward(targets, transfer, leaves):
    counts = level_sizes(leaves)
    offsets = [sum(counts[:height]) for height in range(len(counts))]
    parent = targets[offsets[-1] : offsets[-1] + 1]
    for height in reversed(range(len(counts) - 1)):
        cluster_count = counts[height]
        offset = offsets[height]
        matrices = transfer[offset : offset + cluster_count]
        spread = jnp.repeat(parent, 2, axis=0)
        parent = targets[offset : offset + cluster_count] + jnp.einsum(
            "cji,cjr->cir", matrices, spread, precision=lax.Precision.HIGHEST
        )
    return parent


def shards(
    sources,
    basis_in,
    basis_out,
    transfer,
    coupling,
    coupling_list,
    near_block,
    near_scale,
    near_target,
    near_source,
    near_count,
):
    leaves = sources.shape[0]
    clusters = 2 * leaves - 1
    morton_index = lax.axis_index("morton")
    partial_leaf = jnp.einsum("lkp,lrp->lkr", basis_in, sources, preferred_element_type=jnp.float32)
    whole_rows = lax.all_gather(sources, "slab", axis=2, tiled=True)
    window_sources = extended(whole_rows, (("morton", 0),), leaves)
    leaf_skeleton = lax.psum(partial_leaf, "slab")
    skeletons = upward(leaf_skeleton, transfer)
    window_skeleton = extended(skeletons, (("morton", 0),), clusters)
    top_skeleton = lax.all_gather(skeletons[clusters - 1 :], "morton", axis=0, tiled=True)
    table = jnp.concatenate([window_skeleton, top_skeleton], axis=0)
    owner = coupling_list // clusters
    within = coupling_list % clusters
    table_rows = jnp.where(
        within == clusters - 1, 3 * clusters + owner, (owner - morton_index + 1) * clusters + within
    )
    picked = table[table_rows]
    partial_targets = jnp.einsum(
        "cekj,cejr->ckr", coupling, picked, precision=lax.Precision.HIGHEST
    )
    targets = lax.psum(partial_targets, "slab")
    leaf_field = downward(targets, transfer, leaves).astype(jnp.bfloat16)
    far_field = jnp.einsum(
        "lkr,lkp->lrp", leaf_field, basis_out, preferred_element_type=jnp.float32
    )
    source_rows = near_source - (morton_index - 1) * leaves
    target_rows = near_target - morton_index * leaves
    live_count = near_count[0]
    leaf_ids = jnp.arange(leaves, dtype=jnp.int32)
    slots = near_block.shape[0]
    gathered = window_sources[source_rows]
    products = jnp.einsum("npq,nrq->nrp", near_block, gathered, preferred_element_type=jnp.float32)
    weights = jnp.where(
        jnp.arange(slots, dtype=jnp.int32) < live_count, near_scale, jnp.zeros_like(near_scale)
    )
    selector = (target_rows[None, :] == leaf_ids[:, None]).astype(jnp.float32) * weights[None, :]
    near_field = jnp.einsum("ln,nrp->lrp", selector, products, precision=lax.Precision.HIGHEST)
    return far_field + near_field


def solution(mesh):
    return jax.shard_map(
        shards,
        mesh=mesh,
        in_specs=(
            P("morton", None, "slab"),
            P("morton", None, "slab"),
            P("morton", None, "slab"),
            P("morton", None, None),
            P("morton", "slab", None, None),
            P("morton", "slab"),
            P("morton", "slab", None),
            P("morton"),
            P("morton"),
            P("morton"),
            P("morton"),
        ),
        out_specs=P("morton", None, "slab"),
        check_vma=False,
    )
```

profile of v0, /device:TPU:1, one launch (start us, length us, event | category | flops | bytes accessed | tf_op | source)
XLA Modules:
  0.0 295.5 jit_solution(3250087596092924435)
XLA Ops:
  6.6 0.0 all-reduce.3.cloned.1.call-start
  6.6 1.2 copy.24
  7.8 21.5 %all_gather.7 = bf16[16,32,256]{1,0,2:T(8,128)(2,1)} all-gather(bf16[16,32,32]{1,0,2:T(8,128)(2,1)S(1)} %copy.24), channel_id=1, replica_groups=mesh['morton'=64,'slab'=8] {'slab'}, dimensions={2}, use_global_device_ids=true | all-gather | bytes 294912 | tf_op jit(solution)/shard_map/all_gather | solution.py:71
  29.3 2.7 copy.25
  32.0 2.0 collective-permute-start.2
  33.9 1.3 collective-permute-start.3
  35.3 0.9 fusion.26
  36.1 0.0 all-reduce.3.cloned.1.call-update
  36.1 0.0 all-reduce.5.cloned.1.call-start
  36.2 0.1 copy.23
  36.3 0.1 reshape.35
  37.2 70.4 %all-reduce.3.cloned.1.call-done = f32[16,64,32]{1,2,0:T(8,128)} async-done(((f32[16,64,32]{1,2,0:T(8,128)}), f32[16,64,32]{1,2,0:T(8,128)}) %all-reduce.3.cloned.1.call-update) | async-done | bytes 131088 | tf_op jit(solution)/shard_map/psum | solution.py:73
  107.6 2.1 bitcast_reduce_fusion
  109.6 1.5 bitcast_reduce_fusion.1
  111.1 1.7 constant_dynamic-update-slice_fusion.4
  112.8 0.7 constant_dynamic-update-slice_fusion.3
  113.5 1.2 bitcast_reduce_fusion.2
  114.7 0.6 constant_dynamic-update-slice_fusion.2
  115.3 0.6 constant_dynamic-update-slice_fusion.1
  116.0 1.6 constant_dynamic-update-slice_fusion
  117.6 3.3 %collective-permute-start = (f32[31,64,32]{1,2,0:T(8,128)}, f32[31,64,32]{1,2,0:T(8,128)}, u32[]{:S(2)}, u32[]{:S(2)}) collective-permute-start(f32[31,64,32]{1,2,0:T(8,128)} %get-tuple-element.5), channel_id=1, source_target_pairs={{0,8},{8,16},{16,24},{24,32},{32,40},{40,48},{48,56},{56,64},{64,7... | collective-permute-start | bytes 761864 | tf_op jit(solution)/shard_map/ppermute | solution.py:14
  120.9 1.3 collective-permute-start.1
  122.2 52.2 %all-gather.1 = f32[64,64,32]{1,2,0:T(8,128)} all-gather(f32[1,64,32]{1,2,0:T(8,128)S(1)} %get-tuple-element.6), channel_id=2, replica_groups=mesh['morton'=64,'slab'=8] {'morton'}, dimensions={0}, use_global_device_ids=true | all-gather | bytes 532480 | tf_op jit(solution)/shard_map/all_gather | solution.py:76
  174.4 0.0 collective-permute-done.2
  174.4 0.0 collective-permute-done.3
  174.4 2.1 pad_maximum_fusion
  176.5 3.8 %gather_fusion.1 = bf16[192,32,256]{2,1,0:T(8,128)(2,1)} fusion(bf16[48,32,256]{2,1,0:T(8,128)(2,1)} %pad_maximum_fusion, s32[1024]{0:T(1024)S(1)} %pad_clamp_fusion), kind=kCustom, calls=%fused_computation.1 | custom fusion | bytes 6292224 | tf_op jit(solution)/shard_map/gather | solution.py:97
  180.3 4.5 %fusion.25 = f32[192,32,32]{2,1,0:T(8,128)} fusion(bf16[192,32,256]{2,1,0:T(8,128)(2,1)} %gather_fusion.1, bf16[192,32,256]{2,1,0:T(8,128)(2,1)S(1)} %copy-done), kind=kOutput, calls=%fused_computation.62 | convolution fusion | flops 100663296 | bytes 7077888 | tf_op jit(solution)/shard_map/npq,nrq->nrp/dot_general | solution.py:98
  184.8 1.9 constant_dynamic-update-slice_fusion.12
  186.8 0.7 constant_dynamic-update-slice_fusion.11
  187.5 0.7 constant_dynamic-update-slice_fusion.10
  188.1 0.6 constant_dynamic-update-slice_fusion.9
  188.8 0.6 constant_dynamic-update-slice_fusion.8
  189.4 0.6 constant_dynamic-update-slice_fusion.7
  190.0 1.9 constant_dynamic-update-slice_fusion.6
  191.9 1.1 constant_dynamic-update-slice_fusion.5
  193.0 3.3 %gather_fusion = f32[62,64,32]{1,2,0:T(8,128)} fusion(f32[157,64,32]{1,2,0:T(8,128)} %constant_dynamic-update-slice_fusion.5, s32[1024]{0:T(1024)S(1)} %pad_clamp_fusion.1), kind=kCustom, calls=%fused_computation | custom fusion | bytes 1016056 | tf_op jit(solution)/shard_map/gather | solution.py:83
  196.3 4.5 %convolution_bitcast_fusion = f32[31,64,32]{1,2,0:T(8,128)} fusion(f32[31,2,64,32]{2,3,1,0:T(8,128)} %bitcast.67, f32[31,2,64,64]{3,2,1,0:T(8,128)} %param.15), kind=kOutput, calls=%fused_computation.4 | convolution fusion | flops 97517568 | bytes 1777664 | tf_op jit(solution)/shard_map/cekj,cejr->ckr/dot_general | solution.py:84
  200.8 0.0 all-reduce.5.cloned.1.call-update
  200.9 0.0 copy-start.5
  200.9 5.1 %fusion = f32[16,32,32]{2,0,1:T(8,128)S(1)} fusion(f32[192,32,32]{2,1,0:T(8,128)} %fusion.25, f32[192]{0:T(256)S(1)} %compare_select_fusion.2, s32[192]{0:T(256)S(1)} %broadcast_subtract_fusion), kind=kOutput, calls=%fused_computation.2 | convolution fusion | flops 37754880 | bytes 853504 | tf_op jit(solution)/shard_map/ln,nrp->lrp/dot_general | solution.py:103
  206.0 75.7 %all-reduce.5.cloned.1.call-done = f32[31,64,32]{1,2,0:T(8,128)} async-done(((f32[31,64,32]{1,2,0:T(8,128)}), f32[31,64,32]{1,2,0:T(8,128)}) %all-reduce.5.cloned.1.call-update) | async-done | bytes 253968 | tf_op jit(solution)/shard_map/psum | solution.py:87
  281.7 0.7 slice_bitcast_fusion
  282.5 1.0 fusion.6
  283.5 1.1 fusion.5
  284.7 1.3 fusion.4
  286.0 1.7 fusion.3
  287.7 0.9 convolution_add_fusion
  (30 shorter events, 0.1 us)
Async XLA Ops:
  6.5 173.7 %copy-start = (bf16[192,32,256]{2,1,0:T(8,128)(2,1)S(1)}, bf16[192,32,256]{2,1,0:T(8,128)(2,1)}, u32[]{:S(2)}) copy-start(bf16[192,32,256]{2,1,0:T(8,128)(2,1)} %param.17) | copy-start | bytes 9437188
  6.5 28.7 %copy-start.3 = (bf16[16,32,32]{2,1,0:T(8,128)(2,1)S(1)}, bf16[16,32,32]{2,1,0:T(8,128)(2,1)}, u32[]{:S(2)}) copy-start(bf16[16,32,32]{2,1,0:T(8,128)(2,1)} %param.11) | copy-start | bytes 98308
  6.5 28.7 %copy-start.4 = (bf16[16,64,32]{1,2,0:T(8,128)(2,1)S(1)}, bf16[16,64,32]{1,2,0:T(8,128)(2,1)}, u32[]{:S(2)}) copy-start(bf16[16,64,32]{1,2,0:T(8,128)(2,1)} %param.12) | copy-start | bytes 196612
  6.5 29.7 %copy-start.6 = (s32[31,2]{0,1:T(2,128)S(1)}, s32[31,2]{0,1:T(2,128)}, u32[]{:S(2)}) copy-start(s32[31,2]{0,1:T(2,128)} %param.16) | copy-start | bytes 748
  6.5 30.6 %copy-start.7 = (s32[192]{0:T(256)S(1)}, s32[192]{0:T(256)}, u32[]{:S(2)}) copy-start(s32[192]{0:T(256)} %param.20) | copy-start | bytes 2308
  6.5 30.6 %copy-start.8 = (s32[192]{0:T(256)S(1)}, s32[192]{0:T(256)}, u32[]{:S(2)}) copy-start(s32[192]{0:T(256)} %param.19) | copy-start | bytes 2308
  6.6 30.6 %copy-start.9 = (f32[192]{0:T(256)S(1)}, f32[192]{0:T(256)}, u32[]{:S(2)}) copy-start(f32[192]{0:T(256)} %param.18) | copy-start | bytes 2308
  6.6 101.0 %all-reduce.3.cloned.1.call-start = ((), (), s32[]{:S(2)}) async-start(), calls=%async_computation | async-start | bytes 524288 | tf_op jit(solution)/shard_map/psum | solution.py:73
  32.0 142.4 %collective-permute-start.2 = (bf16[16,32,256]{2,1,0:T(8,128)(2,1)}, bf16[16,32,256]{2,1,0:T(8,128)(2,1)}, u32[]{:S(2)}, u32[]{:S(2)}) collective-permute-start(bf16[16,32,256]{2,1,0:T(8,128)(2,1)} %copy.25), channel_id=1, source_target_pairs={{0,8},{8,16},{16,24},{24,32},{32,40},{40,48},{48,56},{56,64},{64,7... | collective-permute-start | bytes 786440 | tf_op jit(solution)/shard_map/ppermute | solution.py:14
  33.9 140.4 %collective-permute-start.3 = (bf16[16,32,256]{2,1,0:T(8,128)(2,1)}, bf16[16,32,256]{2,1,0:T(8,128)(2,1)}, u32[]{:S(2)}, u32[]{:S(2)}) collective-permute-start(bf16[16,32,256]{2,1,0:T(8,128)(2,1)} %copy.25), channel_id=1, source_target_pairs={{8,0},{16,8},{24,16},{32,24},{40,32},{48,40},{56,48},{64,56},{72,6... | collective-permute-start | bytes 786440 | tf_op jit(solution)/shard_map/ppermute | solution.py:15
  36.1 245.6 %all-reduce.5.cloned.1.call-start = ((), (), s32[]{:S(2)}) async-start(), calls=%async_computation.1 | async-start | bytes 1015808 | tf_op jit(solution)/shard_map/psum | solution.py:87
  117.6 67.2 %collective-permute-start = (f32[31,64,32]{1,2,0:T(8,128)}, f32[31,64,32]{1,2,0:T(8,128)}, u32[]{:S(2)}, u32[]{:S(2)}) collective-permute-start(f32[31,64,32]{1,2,0:T(8,128)} %get-tuple-element.5), channel_id=1, source_target_pairs={{0,8},{8,16},{16,24},{24,32},{32,40},{40,48},{48,56},{56,64},{64,7... | collective-permute-start | bytes 761864 | tf_op jit(solution)/shard_map/ppermute | solution.py:14
  120.9 69.1 %collective-permute-start.1 = (f32[31,64,32]{1,2,0:T(8,128)}, f32[31,64,32]{1,2,0:T(8,128)}, u32[]{:S(2)}, u32[]{:S(2)}) collective-permute-start(f32[31,64,32]{1,2,0:T(8,128)} %get-tuple-element.5), channel_id=1, source_target_pairs={{8,0},{16,8},{24,16},{32,24},{40,32},{48,40},{56,48},{64,56},{72,6... | collective-permute-start | bytes 761864 | tf_op jit(solution)/shard_map/ppermute | solution.py:15
  180.3 6.5 %copy-start.2 = (f32[16,64,32]{1,2,0:T(8,128)S(1)}, f32[16,64,32]{1,2,0:T(8,128)}, u32[]{:S(2)}) copy-start(f32[16,64,32]{1,2,0:T(8,128)} %all-reduce.3.cloned.1.call-done) | copy-start | bytes 393220
  184.8 7.1 %copy-start.1 = (f32[64,64,32]{1,2,0:T(8,128)S(1)}, f32[64,64,32]{1,2,0:T(8,128)}, u32[]{:S(2)}) copy-start(f32[64,64,32]{1,2,0:T(8,128)} %all-gather.1) | copy-start | bytes 1572868
  200.9 86.9 %copy-start.5 = (bf16[16,64,32]{1,2,0:T(8,128)(2,1)S(1)}, bf16[16,64,32]{1,2,0:T(8,128)(2,1)}, u32[]{:S(2)}) copy-start(bf16[16,64,32]{1,2,0:T(8,128)(2,1)} %param.13) | copy-start | bytes 196612
Sparse Core Ops, SparseCore 0:
  36.3 71.2 all-reduce.2
  201.0 80.7 all-reduce.4
where the time goes:
time: 297 us; the launch traced here: 295 us
  waiting for transfers between devices  146 us (49%)
  blocking collectives  73.7 us (25%)
  matrix products  27.5 us (9%)
  local copies, waits for them, and re-layouts  23.8 us (8%)
  between operations  14.3 us (5%)
  starting transfers between devices  7.91 us (3%)
    psum x1, waiting for transfers between devices, shards(): targets = lax.psum(partial_targets, 'slab')  75.7 us
    psum x1, waiting for transfers between devices, shards(): leaf_skeleton = lax.psum(partial_leaf, 'slab')  70.4 us
    all_gather x1, blocking collectives, shards(): lax.all_gather(skeletons[clusters - 1:], 'morton', axis=0, tiled=True)  52.2 us
    all_gather x1, blocking collectives, shards(): whole_rows = lax.all_gather(sources, 'slab', axis=2, tiled=True)  21.5 us
    unnamed x32, local copies, waits for them, and re-layouts  11.9 us
    dot_general x4, matrix products, upward(): jnp.einsum('cij,cjr->cir', matrices, current, precision=lax.Precision.HIG...  6.38 us
  transfers between devices with their start and end apart: 6, of which 2 were waited for; matrix products, arithmetic and copies ran while one was open for 11% of the time, Pallas kernels for 0%

commit v1 on v0

v1 whole, which is shorter than its diff:
```python
import jax
import jax.numpy as jnp
from jax import lax
from jax.experimental import pallas as pl
from jax.experimental.pallas import tpu as pltpu
from jax.sharding import Mesh, PartitionSpec as P

LEAVES = 16
CLUSTERS = 31
RANK = 64
RHS = 32
POINTS = 256
SLABS = 8
PART = POINTS // SLABS
PAIRS = 15
SRC_ROWS = LEAVES * RHS * PART // 128
BASIS_ROWS = LEAVES * PART * RANK // 128
TOP_ROW = SRC_ROWS + BASIS_ROWS
OWNER_ROW = TOP_ROW + RANK
PACKED = OWNER_ROW + 16
TILE_SLOTS = 8
NEAR_CHUNKS = 4
bf16 = jnp.bfloat16
f32 = jnp.float32
MIB = 1024 * 1024
pin = pltpu.with_memory_space_constraint
HBM = pltpu.HBM
NT = (((1,), (1,)), ((), ()))
NN = (((1,), (0,)), ((), ()))


def dot(a, b, dims):
    return lax.dot_general(a, b, dims, preferred_element_type=f32)


def split(x):
    high = x.astype(bf16)
    return high, (x - high.astype(f32)).astype(bf16)


def dot3(a, b, dims):
    a_high, a_low = a
    b_high, b_low = b
    rows = a_high.shape[0]
    both = dot(jnp.concatenate([a_high, a_low], axis=0), b_high, dims)
    return both[:rows] + both[rows:] + dot(a_high, b_low, dims)


def pair_matrices(transfer_ref, i):
    return jnp.concatenate([transfer_ref[2 * i], transfer_ref[2 * i + 1]], axis=1)


def climb(pairs, transfer_ref, keep):
    first = 0
    count = LEAVES // 2
    while True:
        parents = []
        for i in range(first, first + count):
            parts = split(pairs[i])
            keep(i, parts)
            parents.append(dot3(parts, split(pair_matrices(transfer_ref, i)), NT))
        if count == 1:
            return parents[0]
        first = first + count
        count = count // 2
        for i in range(count):
            pairs.append(jnp.concatenate([parents[2 * i], parents[2 * i + 1]], axis=1))


def descend(level, transfer_ref, own):
    first = PAIRS - 1
    while first > 0:
        parents = []
        for pair in level:
            parents.append(pair[:, :RANK])
            parents.append(pair[:, RANK:])
        first = first - len(parents)
        level = []
        for i, parent in enumerate(parents):
            passed = dot3(split(parent), split(pair_matrices(transfer_ref, first + i)), NN)
            level.append(passed if own is None else own(first + i) + passed)
    return level


def leaf_pair(sources, basis):
    product = dot(jnp.concatenate(sources, axis=0), basis, NN)
    left = lax.broadcasted_iota(jnp.int32, (RHS, 128), 1) < RANK
    return jnp.where(left, product[:RHS], product[RHS:])


def fetch(pairs, sems):
    copies = [
        pltpu.make_async_copy(src, dst, sems.at[k]) for k, (src, dst) in enumerate(pairs)
    ]
    for copy in copies:
        copy.start()
    return copies


def pack_kernel(
    list_hbm,
    sources_hbm,
    basis_hbm,
    coupling_hbm,
    out_ref,
    sources_ref,
    basis_ref,
    coupling_ref,
    list_ref,
    in_sem,
):
    copies = fetch(
        (
            (sources_hbm, sources_ref),
            (basis_hbm, basis_ref),
            (coupling_hbm.at[CLUSTERS - 1], coupling_ref),
            (list_hbm, list_ref),
        ),
        in_sem,
    )
    for copy in copies:
        copy.wait()
    owners = [
        lax.shift_right_logical(list_ref[e, CLUSTERS - 1] * 2115, 16) for e in range(2)
    ]
    lane = lax.broadcasted_iota(jnp.int32, (16, 128), 1)
    out_ref[OWNER_ROW : OWNER_ROW + 16, :] = (
        jnp.where(lane == 0, owners[0], owners[1]).astype(f32).astype(bf16)
    )
    for g in range(LEAVES // 4):
        out_ref[g * RHS : (g + 1) * RHS, :] = jnp.concatenate(
            [sources_ref[4 * g + i] for i in range(4)], axis=1
        )
    for i in range(LEAVES // 2):
        start = SRC_ROWS + i * PART
        out_ref[start : start + PART, :] = jnp.concatenate(
            [basis_ref[2 * i], basis_ref[2 * i + 1]], axis=1
        )
    out_ref[TOP_ROW : TOP_ROW + RANK, :] = jnp.concatenate(
        [coupling_ref[0], coupling_ref[1]], axis=1
    ).astype(bf16)


def up_kernel(
    packed_hbm,
    transfer_ref,
    mine_hbm,
    top_hbm,
    matrix_hbm,
    owner_ref,
    sources_ref,
    basis_ref,
    owners_ref,
    mine_ref,
    top_ref,
    in_sem,
    out_sem,
):
    copies = fetch(
        (
            (packed_hbm.at[:, pl.ds(0, SRC_ROWS)], sources_ref),
            (packed_hbm.at[:, pl.ds(SRC_ROWS, BASIS_ROWS)], basis_ref),
            (packed_hbm.at[:, pl.ds(OWNER_ROW, 16)], owners_ref),
            (packed_hbm.at[:, pl.ds(TOP_ROW, RANK)], matrix_hbm),
        ),
        in_sem,
    )
    copies[0].wait()
    for g in range(LEAVES // 4):
        tiles = [sources_ref[s, g * RHS : (g + 1) * RHS, :] for s in range(SLABS)]
        for i in range(4):
            mine_ref[4 * g + i] = jnp.concatenate(
                [t[:, i * PART : (i + 1) * PART] for t in tiles], axis=1
            )
    rows = pl.ds(0, LEAVES)
    out_rows = pltpu.make_async_copy(mine_ref.at[rows], mine_hbm.at[rows], out_sem.at[0])
    out_rows.start()
    copies[1].wait()
    pairs = []
    for i in range(LEAVES // 2):
        basis = jnp.concatenate(
            [basis_ref[s, i * PART : (i + 1) * PART, :] for s in range(SLABS)], axis=0
        )
        pairs.append(leaf_pair([mine_ref[2 * i], mine_ref[2 * i + 1]], basis))

    def keep(i, parts):
        mine_ref[LEAVES + i] = jnp.concatenate(parts, axis=1)

    top = climb(pairs, transfer_ref, keep).astype(bf16)
    rows = pl.ds(LEAVES, PAIRS)
    out_pairs = pltpu.make_async_copy(mine_ref.at[rows], mine_hbm.at[rows], out_sem.at[1])
    out_pairs.start()
    row = jnp.concatenate([top[: RHS // 2], top[RHS // 2 :]], axis=1)
    top_ref[...] = jnp.broadcast_to(row[None], top_ref.shape)
    out_top = pltpu.make_async_copy(top_ref, top_hbm, out_sem.at[2])
    out_top.start()
    copies[2].wait()
    for s in range(SLABS):
        owner_ref[s : s + 1, :] = owners_ref[s].astype(f32)[:1].astype(jnp.int32)
    out_rows.wait()
    out_pairs.wait()
    out_top.wait()
    copies[3].wait()


def top_kernel(
    owner_hbm, tops_hbm, matrix_hbm, transfer_ref, out_ref, owner_ref, tops_ref, matrix_ref, in_sem
):
    copies = fetch(
        (
            (tops_hbm, tops_ref),
            (matrix_hbm, matrix_ref),
            (owner_hbm, owner_ref),
        ),
        in_sem,
    )
    for copy in copies:
        copy.wait()

    def top_of(s, e):
        block = tops_ref[owner_ref[s, e]]
        return jnp.concatenate([block[:, :RANK], block[:, RANK:]], axis=0)

    top = jnp.zeros((RHS, RANK), f32)
    for s in range(SLABS):
        picked = jnp.concatenate([top_of(s, 0), top_of(s, 1)], axis=1)
        top = top + dot(picked, matrix_ref[s], NT)
    matrices = split(pair_matrices(transfer_ref, PAIRS - 1))
    level = descend([dot3(split(top), matrices, NN)], transfer_ref, None)
    for i in range(LEAVES // 2):
        out_ref[i] = level[i]


def field_kernel(
    list_hbm,
    mine_hbm,
    received_hbm,
    swapped_hbm,
    transfer_ref,
    coupling_ref,
    leaf_hbm,
    list_ref,
    window_ref,
    leaf_ref,
    in_sem,
    out_sem,
):
    copies = fetch(
        [
            (hbm.at[pl.ds(LEAVES, PAIRS)], window_ref.at[pl.ds(k * PAIRS, PAIRS)])
            for k, hbm in zip(window_places(), (mine_hbm, received_hbm, swapped_hbm))
        ]
        + [(list_hbm, list_ref)],
        in_sem,
    )
    left = lax.broadcasted_iota(jnp.int32, (RHS, 128), 1) < RANK
    first_cluster = morton_index() * CLUSTERS - CLUSTERS
    for copy in copies:
        copy.wait()

    def swapped(x):
        return jnp.concatenate([x[:, RANK:], x[:, :RANK]], axis=1)

    def pick(g, e):
        local = list_ref[e, g] - first_cluster
        owner = (local >= CLUSTERS).astype(jnp.int32) + (local >= 2 * CLUSTERS).astype(
            jnp.int32
        )
        cluster = local - owner * CLUSTERS
        pair = lax.shift_right_logical(cluster, 1)
        block = window_ref[owner * PAIRS + pair]
        high, low = block[:, :128], block[:, 128:]
        here = (cluster - 2 * pair) == e
        return jnp.where(here, high, swapped(high)), jnp.where(here, low, swapped(low))

    def coupled(g):
        matrices = split(
            jnp.concatenate([coupling_ref[g, 0], coupling_ref[g, 1]], axis=1)
        )
        (high0, low0), (high1, low1) = pick(g, 0), pick(g, 1)
        picked = (jnp.where(left, high0, high1), jnp.where(left, low0, low1))
        return dot3(picked, matrices, NT)

    def own(i):
        return jnp.concatenate([coupled(2 * i), coupled(2 * i + 1)], axis=1)

    level = descend([own(PAIRS - 1)], transfer_ref, own)
    for i in range(LEAVES // 2):
        leaf_ref[i * RHS : (i + 1) * RHS, :] = level[i].astype(bf16)
    for copy in fetch([(leaf_ref, leaf_hbm.at[s]) for s in range(SLABS)], out_sem):
        copy.wait()


def near_kernel(
    scale_hbm,
    target_hbm,
    source_hbm,
    count_hbm,
    mine_hbm,
    received_hbm,
    swapped_hbm,
    near_hbm,
    out_ref,
    scale_ref,
    target_ref,
    source_ref,
    count_ref,
    window_ref,
    near_ref,
    product_ref,
    in_sem,
):
    chunk = near_ref.shape[0] // NEAR_CHUNKS
    copies = fetch(
        [
            (scale_hbm, scale_ref),
            (target_hbm, target_ref),
            (source_hbm, source_ref),
            (count_hbm, count_ref),
        ]
        + [
            (hbm.at[pl.ds(0, LEAVES)], window_ref.at[pl.ds(k * LEAVES, LEAVES)])
            for k, hbm in zip(window_places(), (mine_hbm, received_hbm, swapped_hbm))
        ]
        + [
            (near_hbm.at[pl.ds(k * chunk, chunk)], near_ref.at[pl.ds(k * chunk, chunk)])
            for k in range(NEAR_CHUNKS)
        ],
        in_sem,
    )
    out_ref[...] = jnp.zeros_like(out_ref)
    morton = morton_index()
    first_source = (morton - 1) * LEAVES
    first_target = morton * LEAVES
    for copy in copies[:-NEAR_CHUNKS]:
        copy.wait()
    live = count_ref[0]

    def tile(t, carry):
        base = t * TILE_SLOTS
        for k in range(TILE_SLOTS):
            slot = base + k
            row = source_ref[slot] - first_source
            product_ref[k] = dot(window_ref[row], near_ref[slot], NT)
        for k in range(TILE_SLOTS):
            slot = base + k
            target = target_ref[slot] - first_target
            weight = jnp.where(slot < live, scale_ref[slot], 0.0)
            out_ref[target] += weight * product_ref[k]
        return carry

    tiles = (live + TILE_SLOTS - 1) // TILE_SLOTS
    step = chunk // TILE_SLOTS
    for k in range(NEAR_CHUNKS):
        copies[k - NEAR_CHUNKS].wait()
        lax.fori_loop(k * step, jnp.clip(tiles, k * step, (k + 1) * step), tile, 0)


def far_kernel(parts_hbm, extra_ref, basis_ref, near_ref, out_ref, parts_ref, sem):
    half = LEAVES // 4 * RHS
    copies = fetch(
        [
            (parts_hbm.at[:, pl.ds(k * half, half)], parts_ref.at[:, pl.ds(k * half, half)])
            for k in range(2)
        ],
        sem,
    )
    for i in range(LEAVES // 2):
        if i % (LEAVES // 4) == 0:
            copies[i // (LEAVES // 4)].wait()
        rows = pl.ds(i * RHS, RHS)
        total = extra_ref[i]
        for s in range(SLABS):
            total = total + parts_ref[s, rows, :].astype(f32)
        high, low = split(total)
        both = jnp.concatenate([high, low], axis=0)
        for k in range(2):
            leaf = 2 * i + k
            product = dot(both[:, k * RANK : (k + 1) * RANK], basis_ref[leaf], NT)
            out_ref[leaf] = near_ref[leaf] + (product[:RHS] + product[RHS:])


def window_places():
    odd = lax.axis_index("slab") % 2
    return 1, 2 * odd, 2 - 2 * odd


def morton_index():
    return lax.axis_index(("z", "y"))


def vmem(n):
    return [pl.BlockSpec(memory_space=pltpu.VMEM)] * n


def smem(n):
    return [pl.BlockSpec(memory_space=pltpu.SMEM)] * n


def hbm(n):
    return [pl.BlockSpec(memory_space=pltpu.HBM)] * n


def shards(
    sources,
    basis_in,
    basis_out,
    transfer,
    coupling,
    coupling_list,
    near_block,
    near_scale,
    near_target,
    near_source,
    near_count,
):
    height, columns = lax.axis_size("z"), lax.axis_size("y")
    count = height * columns
    slots = near_block.shape[0]
    listed = coupling_list.T
    dma = pltpu.SemaphoreType.DMA

    def call(kernel, name, outs, in_specs, out_specs, scratch, limit=40, **params):
        return pl.pallas_call(
            kernel,
            out_shape=tuple(
                out[2](*out[:2]) if out[2:] else jax.ShapeDtypeStruct(*out)
                for out in outs
            ),
            in_specs=in_specs,
            out_specs=tuple(out_specs),
            scratch_shapes=scratch,
            compiler_params=pltpu.CompilerParams(vmem_limit_bytes=limit * MIB),
            name=name,
            **params,
        )

    (packed,) = call(
        pack_kernel,
        "pack",
        [((PACKED, 128), bf16)],
        hbm(4),
        vmem(1),
        [
            pltpu.VMEM(sources.shape, bf16),
            pltpu.VMEM((LEAVES, PART, RANK), bf16),
            pltpu.VMEM(coupling.shape[1:], f32),
            pltpu.SMEM(listed.shape, jnp.int32),
            dma((4,)),
        ],
        limit=56,
    )(
        pin(listed, HBM),
        pin(sources, HBM),
        pin(jnp.swapaxes(basis_in, 1, 2), HBM),
        pin(coupling, HBM),
    )
    gathered = lax.all_gather(packed, "slab")
    mine, top, matrix, owner = call(
        up_kernel,
        "up",
        [
            ((LEAVES + PAIRS, RHS, POINTS), bf16, HBM),
            ((count, RHS // 2, 128), bf16, HBM),
            ((SLABS, RANK, 128), bf16, HBM),
            ((SLABS, 128), jnp.int32),
        ],
        hbm(1) + vmem(1),
        hbm(3) + vmem(1),
        [
            pltpu.VMEM((SLABS, SRC_ROWS, 128), bf16),
            pltpu.VMEM((SLABS, BASIS_ROWS, 128), bf16),
            pltpu.VMEM((SLABS, 16, 128), bf16),
            pltpu.VMEM((LEAVES + PAIRS, RHS, POINTS), bf16),
            pltpu.VMEM((count, RHS // 2, 128), bf16),
            dma((4,)),
            dma((3,)),
        ],
    )(gathered, transfer)
    moves = []
    for m in range(count):
        for s in range(SLABS):
            to = m + 1 - 2 * (s % 2)
            if 0 <= to < count:
                moves.append((m * SLABS + s, to * SLABS + s))
    received = lax.ppermute(mine, ("z", "y", "slab"), moves)
    swapped = lax.ppermute(received, "slab", [(s, s ^ 1) for s in range(SLABS)])
    mine, received, swapped = pin(mine, HBM), pin(received, HBM), pin(swapped, HBM)
    tops = lax.all_to_all(top, ("z", "y"), 0, 0)
    (leaf,) = call(
        field_kernel,
        "field",
        [
            ((SLABS, LEAVES // 2 * RHS, 128), bf16, HBM),
        ],
        hbm(4) + vmem(2),
        hbm(1),
        [
            pltpu.SMEM(listed.shape, jnp.int32),
            pltpu.VMEM((3 * PAIRS, RHS, 256), bf16),
            pltpu.VMEM((LEAVES // 2 * RHS, 128), bf16),
            dma((4,)),
            dma((SLABS,)),
        ],

    )(
        listed,
        mine,
        received,
        swapped,
        transfer,
        coupling,
    )
    parts = lax.all_to_all(leaf, "slab", 0, 0)
    (near,) = call(
        near_kernel,
        "near",
        [((LEAVES, RHS, PART), f32)],
        hbm(8),
        vmem(1),
        [
            pltpu.SMEM((slots,), f32),
            pltpu.SMEM((slots,), jnp.int32),
            pltpu.SMEM((slots,), jnp.int32),
            pltpu.SMEM((1,), jnp.int32),
            pltpu.VMEM((3 * LEAVES, RHS, POINTS), bf16),
            pltpu.VMEM((slots, PART, POINTS), bf16),
            pltpu.VMEM((TILE_SLOTS, RHS, PART), f32),
            dma((7 + NEAR_CHUNKS,)),
        ],
    )(
        near_scale,
        near_target,
        near_source,
        near_count,
        mine,
        received,
        swapped,
        pin(near_block, HBM),
    )
    (extra,) = call(
        top_kernel,
        "top",
        [((LEAVES // 2, RHS, 128), f32)],
        hbm(3) + vmem(1),
        vmem(1),
        [
            pltpu.SMEM((SLABS, 128), jnp.int32),
            pltpu.VMEM((count, RHS // 2, 128), bf16),
            pltpu.VMEM((SLABS, RANK, 128), bf16),
            dma((3,)),
        ],
    )(owner, tops, matrix, transfer)
    (out,) = call(
        far_kernel,
        "far",
        [((LEAVES, RHS, PART), f32)],
        hbm(1) + vmem(3),
        vmem(1),
        [pltpu.VMEM((SLABS, LEAVES // 2 * RHS, 128), bf16), dma((2,))],
    )(parts, extra, jnp.swapaxes(basis_out, 1, 2), near)
    return out


COLUMNS = 8


def solution(mesh):
    grid = mesh.devices.reshape(-1, COLUMNS, mesh.shape["slab"])
    morton = ("z", "y")
    return jax.shard_map(
        shards,
        mesh=Mesh(grid, ("z", "y", "slab")),
        in_specs=(
            P(morton, None, "slab"),
            P(morton, None, "slab"),
            P(morton, None, "slab"),
            P(morton, None, None),
            P(morton, "slab", None, None),
            P(morton, "slab"),
            P(morton, "slab", None),
            P(morton),
            P(morton),
            P(morton),
            P(morton),
        ),
        out_specs=P(morton, None, "slab"),
        check_vma=False,
    )
```

time: 297 us -> 68.9 us (0.23)
  waiting for transfers between devices: 146 us -> 8.3 us
  blocking collectives: 73.7 us -> 20.6 us
  matrix products: 27.5 us -> 0 us
  local copies, waits for them, and re-layouts: 23.8 us -> 0.84 us
  starting transfers between devices: 7.91 us -> 23.1 us
  Pallas kernels: 0 us -> 14.9 us
  between operations: 14.3 us -> 0.8 us
    psum x2 -> x0, waiting for transfers between devices: 146 us -> none  [the longest x1 75.7 us: shards(): targets = lax.psum(partial_targets, 'slab')]
    all_gather x2 -> x1, blocking collectives: 73.7 us -> 20.6 us  [shards(): gathered = lax.all_gather(packed, 'slab')]
    dot_general x13 -> x0, matrix products: 27.5 us -> none  [the longest x4 6.38 us: upward(): jnp.einsum('cij,cjr->cir', matrices, current, precision=lax.Precision.HIG...]
    all_to_all x0 -> x2, starting transfers between devices: none -> 18.9 us  [the longest x1 12.1 us: shards(): tops = lax.all_to_all(top, ('z', 'y'), 0, 0)]
    pallas_call x0 -> x6, Pallas kernels: none -> 14.9 us  [the longest x1 4.1 us: shards(): call(near_kernel, 'near', [((LEAVES, RHS, PART), f32)], hbm(8), vmem(1),...]
    unnamed x32 -> x18, local copies, waits for them, and re-layouts: 11.9 us -> 0.84 us
    gather x2 -> x0, local copies, waits for them, and re-layouts: 7.13 us -> none  [the longest x1 3.81 us: shards(): gathered = window_sources[source_rows]]
    all_to_all x0 -> x2, waiting for transfers between devices: none -> 6.59 us  [the longest x1 3.85 us: shards(): tops = lax.all_to_all(top, ('z', 'y'), 0, 0)]
  transfers between devices with their start and end apart: 6 -> 4, of which waited for: 2 -> 3; matrix products, arithmetic and copies ran while one was open for 11% -> 0% of each run, Pallas kernels for 0% -> 14%
where the time goes in v1:
time: 68.9 us; the launch traced here: 68.6 us
  starting transfers between devices  23.1 us (34%)
  blocking collectives  20.6 us (30%)
  Pallas kernels  14.9 us (22%)
  waiting for transfers between devices  8.3 us (12%)
  local copies, waits for them, and re-layouts  0.84 us (1%)
  between operations  0.8 us (1%)
    all_gather x1, blocking collectives, shards(): gathered = lax.all_gather(packed, 'slab')  20.6 us
    all_to_all x1, starting transfers between devices, shards(): tops = lax.all_to_all(top, ('z', 'y'), 0, 0)  12.1 us
    all_to_all x1, starting transfers between devices, shards(): parts = lax.all_to_all(leaf, 'slab', 0, 0)  6.86 us
    pallas_call x1, Pallas kernels, shards(): call(near_kernel, 'near', [((LEAVES, RHS, PART), f32)], hbm(8), vmem(1),...  4.1 us
    all_to_all x1, waiting for transfers between devices, shards(): tops = lax.all_to_all(top, ('z', 'y'), 0, 0)  3.85 us
    pallas_call x1, Pallas kernels, shards(): call(field_kernel, 'field', [((SLABS, LEAVES // 2 * RHS, 128), bf16, HBM)...  3.52 us
    ppermute x1, starting transfers between devices, shards(): swapped = lax.ppermute(received, 'slab', [(s, s ^ 1) for s in range(SLABS)])  2.87 us
    all_to_all x1, waiting for transfers between devices, shards(): parts = lax.all_to_all(leaf, 'slab', 0, 0)  2.74 us
  transfers between devices with their start and end apart: 4, of which 3 were waited for; matrix products, arithmetic and copies ran while one was open for 0% of the time, Pallas kernels for 14%

profile of v1, /device:TPU:1, one launch (start us, length us, event | category | flops | bytes accessed | tf_op | source)
XLA Modules:
  0.0 68.6 jit_solution(3960368148304138808)
XLA Ops:
  0.0 0.0 copy-start.1
  0.0 0.0 copy-start.4
  0.0 0.0 copy-start
  0.0 1.9 %pack.1 = bf16[464,128]{1,0:T(8,128)(2,1)} custom-call(s32[2,31]{1,0:T(2,128)} %bitcast.6, bf16[16,32,32]{2,1,0:T(8,128)(2,1)} %sources_hbm.1, bf16[16,32,64]{2,1,0:T(8,128)(2,1)} %bitcast.8, f32[31,2,64,64]{3,2,1,0:T(8,128)} %coupling_ref.1), custom_call_target="tpu_custom_call" | custom-call | tf_op jit(solution)/shard_map/pack/pallas_call | solution.py:438
  1.9 20.6 %all-gather = bf16[3712,128]{1,0:T(8,128)(2,1)S(1)} all-gather(bf16[464,128]{1,0:T(8,128)(2,1)} %pack.1), channel_id=2, replica_groups=mesh['z'=8,'y'=8,'slab'=8] {'slab'}, dimensions={0}, use_global_device_ids=true | all-gather | bytes 1069056 | tf_op jit(solution)/shard_map/all_gather | solution.py:458
  22.5 0.0 copy-done
  22.5 2.2 %up.1 = (bf16[31,32,256]{2,1,0:T(8,128)(2,1)}, bf16[64,16,128]{2,1,0:T(8,128)(2,1)}, bf16[8,64,128]{2,1,0:T(8,128)(2,1)}, s32[8,128]{1,0:T(8,128)S(1)}) custom-call(bf16[8,464,128]{2,1,0:T(8,128)(2,1)S(1)} %bitcast.4, f32[30,64,64]{2,1,0:T(8,128)S(1)} %copy-done), custom_call_target="tpu_custom_call" | custom-call | tf_op jit(solution)/shard_map/up/pallas_call | solution.py:459
  24.8 1.3 %collective-permute-start = (bf16[31,32,256]{2,1,0:T(8,128)(2,1)}, bf16[31,32,256]{2,1,0:T(8,128)(2,1)}, u32[]{:S(2)}, u32[]{:S(2)}) collective-permute-start(bf16[31,32,256]{2,1,0:T(8,128)(2,1)} %get-tuple-element.9.mine_hbm), channel_id=1, source_target_pairs={{0,8},{2,10},{4,12},{6,14},{8,16},{9,1},{10,18},{11,3},{12,20},{13... | collective-permute-start | bytes 1523720 | tf_op jit(solution)/shard_map/ppermute | solution.py:486
  26.1 12.1 %all-to-all-start.1 = ((bf16[64,16,128]{2,1,0:T(8,128)(2,1)}), bf16[64,16,128]{2,1,0:T(8,128)(2,1)S(1)}, u32[]{:S(2)}, u32[]{:S(2)}) async-start(bf16[64,16,128]{2,1,0:T(8,128)(2,1)} %get-tuple-element.11), calls=%async_computation.1 | async-start | bytes 524288 | tf_op jit(solution)/shard_map/all_to_all | solution.py:489
  38.2 0.0 copy-start.3
  38.2 0.0 copy-start.5
  38.2 0.0 copy-start.6
  38.2 0.0 copy-start.7
  38.2 0.0 collective-permute-done.received_hbm
  38.2 2.9 %collective-permute-start.1 = (bf16[31,32,256]{2,1,0:T(8,128)(2,1)}, bf16[31,32,256]{2,1,0:T(8,128)(2,1)S(1)}, u32[]{:S(2)}, u32[]{:S(2)}) collective-permute-start(bf16[31,32,256]{2,1,0:T(8,128)(2,1)} %collective-permute-done.received_hbm), channel_id=1, source_target_pairs={{0,1},{1,0},{2,3},{3,2},{4,5},{5,4},{6,7},{7,6},{8,9},{9,8},{10,11... | collective-permute-start | bytes 1523720 | tf_op jit(solution)/shard_map/ppermute | solution.py:487
  41.1 1.7 %collective-permute-done.1.swapped_hbm = bf16[31,32,256]{2,1,0:T(8,128)(2,1)S(1)} collective-permute-done((bf16[31,32,256]{2,1,0:T(8,128)(2,1)}, bf16[31,32,256]{2,1,0:T(8,128)(2,1)S(1)}, u32[]{:S(2)}, u32[]{:S(2)}) %collective-permute-start.1) | collective-permute-done | bytes 507936 | tf_op jit(solution)/shard_map/ppermute | solution.py:487
  42.8 0.0 copy-start.8
  42.8 0.8 %copy-done.8 = bf16[31,32,256]{2,1,0:T(8,128)(2,1)} copy-done((bf16[31,32,256]{2,1,0:T(8,128)(2,1)}, bf16[31,32,256]{2,1,0:T(8,128)(2,1)S(1)}, u32[]{:S(2)}) %copy-start.8) | copy-done | bytes 507928
  43.6 0.0 copy-done.1
  43.6 0.0 copy-done.4
  43.6 3.5 %field.1 = bf16[8,256,128]{2,1,0:T(8,128)(2,1)} custom-call(s32[2,31]{1,0:T(2,128)S(1)} %bitcast.7, bf16[31,32,256]{2,1,0:T(8,128)(2,1)} %get-tuple-element.9.mine_hbm, bf16[31,32,256]{2,1,0:T(8,128)(2,1)} %collective-permute-done.received_hbm, bf16[31,32,256]{2,1,0:T(8,128)(2,1)} %copy-done.8, f32[30,64,64]{2,1,0:T(8,128)S(1)} %copy-done, ...), custom_call_target="tpu_custom_call" | custom-call | tf_op jit(solution)/shard_map/field/pallas_call | solution.py:490
  47.1 3.9 %all-to-all-done.1.tops_hbm = bf16[64,16,128]{2,1,0:T(8,128)(2,1)S(1)} async-done(((bf16[64,16,128]{2,1,0:T(8,128)(2,1)}), bf16[64,16,128]{2,1,0:T(8,128)(2,1)S(1)}, u32[]{:S(2)}, u32[]{:S(2)}) %all-to-all-start.1) | async-done | bytes 262176 | tf_op jit(solution)/shard_map/all_to_all | solution.py:489
  51.0 6.9 %all-to-all-start = ((bf16[8,256,128]{2,1,0:T(8,128)(2,1)}), bf16[8,256,128]{2,1,0:T(8,128)(2,1)S(1)}, u32[]{:S(2)}, u32[]{:S(2)}) async-start(bf16[8,256,128]{2,1,0:T(8,128)(2,1)} %field.1), calls=%async_computation | async-start | bytes 1048576 | tf_op jit(solution)/shard_map/all_to_all | solution.py:514
  58.5 0.0 copy-done.3
  58.5 0.0 copy-start.2
  58.5 1.9 %top.1.extra_ref = f32[8,32,128]{2,1,0:T(8,128)S(1)} custom-call(s32[8,128]{1,0:T(8,128)S(1)} %get-tuple-element.10.owner_hbm, bf16[64,16,128]{2,1,0:T(8,128)(2,1)S(1)} %all-to-all-done.1.tops_hbm, bf16[8,64,128]{2,1,0:T(8,128)(2,1)S(1)} %copy-done.3, f32[30,64,64]{2,1,0:T(8,128)S(1)} %copy-done), custom_call_target="tpu_custom_call" | custom-call | tf_op jit(solution)/shard_map/top/pallas_call | solution.py:541
  60.5 0.0 copy-done.5
  60.5 0.0 copy-done.6
  60.5 0.0 copy-done.7
  60.5 4.1 %near.1.near_ref = f32[16,32,32]{2,1,0:T(8,128)S(1)} custom-call(f32[192]{0:T(256)S(1)} %copy-done.5, s32[192]{0:T(256)S(1)} %copy-done.6, s32[192]{0:T(256)S(1)} %copy-done.7, s32[1]{0:T(128)S(6)} %copy.12.count_hbm, bf16[31,32,256]{2,1,0:T(8,128)(2,1)} %get-tuple-element.9.mine_hbm, bf16[31,32,256]{2,1,0:T(8,128)(2,1)} %collective-permute-done.received_hbm, ...), custom_call_target="tpu_custom_call" | custom-call | tf_op jit(solution)/shard_map/near/pallas_call | solution.py:515
  64.6 2.7 %all-to-all-done.parts_hbm = bf16[8,256,128]{2,1,0:T(8,128)(2,1)S(1)} async-done(((bf16[8,256,128]{2,1,0:T(8,128)(2,1)}), bf16[8,256,128]{2,1,0:T(8,128)(2,1)S(1)}, u32[]{:S(2)}, u32[]{:S(2)}) %all-to-all-start) | async-done | bytes 524320 | tf_op jit(solution)/shard_map/all_to_all | solution.py:514
  67.3 0.0 copy-done.2
  67.3 1.2 %far.1 = f32[16,32,32]{2,1,0:T(8,128)} custom-call(bf16[8,256,128]{2,1,0:T(8,128)(2,1)S(1)} %all-to-all-done.parts_hbm, f32[8,32,128]{2,1,0:T(8,128)S(1)} %top.1.extra_ref, bf16[16,32,64]{2,1,0:T(8,128)(2,1)S(1)} %bitcast.5, f32[16,32,32]{2,1,0:T(8,128)S(1)} %near.1.near_ref), custom_call_target="tpu_custom_call" | custom-call | tf_op jit(solution)/shard_map/far/pallas_call | solution.py:554
Async XLA Ops:
  0.0 43.6 %copy-start.1 = (f32[31,2,64,64]{3,2,1,0:T(8,128)S(1)}, f32[31,2,64,64]{3,2,1,0:T(8,128)}, u32[]{:S(2)}) copy-start(f32[31,2,64,64]{3,2,1,0:T(8,128)} %coupling_ref.1) | copy-start | bytes 3047428
  0.0 43.6 %copy-start.4 = (s32[31,2]{0,1:T(2,128)S(1)}, s32[31,2]{0,1:T(2,128)}, u32[]{:S(2)}) copy-start(s32[31,2]{0,1:T(2,128)} %param.16) | copy-start | bytes 748
  0.0 22.5 %copy-start = (f32[30,64,64]{2,1,0:T(8,128)S(1)}, f32[30,64,64]{2,1,0:T(8,128)}, u32[]{:S(2)}) copy-start(f32[30,64,64]{2,1,0:T(8,128)} %transfer_ref.5) | copy-start | bytes 1474564
  24.8 13.4 %collective-permute-start = (bf16[31,32,256]{2,1,0:T(8,128)(2,1)}, bf16[31,32,256]{2,1,0:T(8,128)(2,1)}, u32[]{:S(2)}, u32[]{:S(2)}) collective-permute-start(bf16[31,32,256]{2,1,0:T(8,128)(2,1)} %get-tuple-element.9.mine_hbm), channel_id=1, source_target_pairs={{0,8},{2,10},{4,12},{6,14},{8,16},{9,1},{10,18},{11,3},{12,20},{13... | collective-permute-start | bytes 1523720 | tf_op jit(solution)/shard_map/ppermute | solution.py:486
  26.1 24.9 %all-to-all-start.1 = ((bf16[64,16,128]{2,1,0:T(8,128)(2,1)}), bf16[64,16,128]{2,1,0:T(8,128)(2,1)S(1)}, u32[]{:S(2)}, u32[]{:S(2)}) async-start(bf16[64,16,128]{2,1,0:T(8,128)(2,1)} %get-tuple-element.11), calls=%async_computation.1 | async-start | bytes 524288 | tf_op jit(solution)/shard_map/all_to_all | solution.py:489
  38.2 20.3 %copy-start.3 = (bf16[8,64,128]{2,1,0:T(8,128)(2,1)S(1)}, bf16[8,64,128]{2,1,0:T(8,128)(2,1)}, u32[]{:S(2)}) copy-start(bf16[8,64,128]{2,1,0:T(8,128)(2,1)} %get-tuple-element.12.matrix_hbm) | copy-start | bytes 393220
  38.2 22.3 %copy-start.5 = (f32[192]{0:T(256)S(1)}, f32[192]{0:T(256)}, u32[]{:S(2)}) copy-start(f32[192]{0:T(256)} %scale_hbm.1) | copy-start | bytes 2308
  38.2 22.3 %copy-start.6 = (s32[192]{0:T(256)S(1)}, s32[192]{0:T(256)}, u32[]{:S(2)}) copy-start(s32[192]{0:T(256)} %target_hbm.1) | copy-start | bytes 2308
  38.2 22.3 %copy-start.7 = (s32[192]{0:T(256)S(1)}, s32[192]{0:T(256)}, u32[]{:S(2)}) copy-start(s32[192]{0:T(256)} %source_hbm.1) | copy-start | bytes 2308
  38.2 4.6 %collective-permute-start.1 = (bf16[31,32,256]{2,1,0:T(8,128)(2,1)}, bf16[31,32,256]{2,1,0:T(8,128)(2,1)S(1)}, u32[]{:S(2)}, u32[]{:S(2)}) collective-permute-start(bf16[31,32,256]{2,1,0:T(8,128)(2,1)} %collective-permute-done.received_hbm), channel_id=1, source_target_pairs={{0,1},{1,0},{2,3},{3,2},{4,5},{5,4},{6,7},{7,6},{8,9},{9,8},{10,11... | collective-permute-start | bytes 1523720 | tf_op jit(solution)/shard_map/ppermute | solution.py:487
  42.8 0.8 %copy-start.8 = (bf16[31,32,256]{2,1,0:T(8,128)(2,1)}, bf16[31,32,256]{2,1,0:T(8,128)(2,1)S(1)}, u32[]{:S(2)}) copy-start(bf16[31,32,256]{2,1,0:T(8,128)(2,1)S(1)} %collective-permute-done.1.swapped_hbm) | copy-start | bytes 1523716
  51.0 16.3 %all-to-all-start = ((bf16[8,256,128]{2,1,0:T(8,128)(2,1)}), bf16[8,256,128]{2,1,0:T(8,128)(2,1)S(1)}, u32[]{:S(2)}, u32[]{:S(2)}) async-start(bf16[8,256,128]{2,1,0:T(8,128)(2,1)} %field.1), calls=%async_computation | async-start | bytes 1048576 | tf_op jit(solution)/shard_map/all_to_all | solution.py:514
  58.5 8.8 %copy-start.2 = (bf16[16,64,32]{1,2,0:T(8,128)(2,1)S(1)}, bf16[16,64,32]{1,2,0:T(8,128)(2,1)}, u32[]{:S(2)}) copy-start(bf16[16,64,32]{1,2,0:T(8,128)(2,1)} %param.13) | copy-start | bytes 196612

commit v2 on v1

--- a/solution.py
+++ b/solution.py
@@ -13,6 +13,8 @@
 SLABS = 8
 PART = POINTS // SLABS
 PAIRS = 15
+HALF = 15
+LEVELS = ((0, 8), (16, 4), (24, 2), (28, 1))
 SRC_ROWS = LEAVES * RHS * PART // 128
 BASIS_ROWS = LEAVES * PART * RANK // 128
 TOP_ROW = SRC_ROWS + BASIS_ROWS
@@ -67,7 +69,7 @@
             pairs.append(jnp.concatenate([parents[2 * i], parents[2 * i + 1]], axis=1))
 
 
-def descend(level, transfer_ref, own):
+def descend(level, transfer_ref):
     first = PAIRS - 1
     while first > 0:
         parents = []
@@ -78,7 +80,7 @@
         level = []
         for i, parent in enumerate(parents):
             passed = dot3(split(parent), split(pair_matrices(transfer_ref, first + i)), NN)
-            level.append(passed if own is None else own(first + i) + passed)
+            level.append(passed)
     return level
 
 
@@ -102,12 +104,18 @@
     sources_hbm,
     basis_hbm,
     coupling_hbm,
+    out_hbm,
+    share_hbm,
     out_ref,
+    share_ref,
     sources_ref,
     basis_ref,
     coupling_ref,
+    half_ref,
     list_ref,
     in_sem,
+    half_sem,
+    out_sem,
 ):
     copies = fetch(
         (
@@ -118,15 +126,15 @@
         ),
         in_sem,
     )
+    halves = fetch(
+        [
+            (coupling_hbm.at[pl.ds(source, count)], half_ref.at[pl.ds(place, count)])
+            for place, source, count in half_of(1 - lax.axis_index("slab") % 2)
+        ],
+        half_sem,
+    )
     for copy in copies:
         copy.wait()
-    owners = [
-        lax.shift_right_logical(list_ref[e, CLUSTERS - 1] * 2115, 16) for e in range(2)
-    ]
-    lane = lax.broadcasted_iota(jnp.int32, (16, 128), 1)
-    out_ref[OWNER_ROW : OWNER_ROW + 16, :] = (
-        jnp.where(lane == 0, owners[0], owners[1]).astype(f32).astype(bf16)
-    )
     for g in range(LEAVES // 4):
         out_ref[g * RHS : (g + 1) * RHS, :] = jnp.concatenate(
             [sources_ref[4 * g + i] for i in range(4)], axis=1
@@ -139,6 +147,27 @@
     out_ref[TOP_ROW : TOP_ROW + RANK, :] = jnp.concatenate(
         [coupling_ref[0], coupling_ref[1]], axis=1
     ).astype(bf16)
+    row = lax.broadcasted_iota(jnp.int32, (16, 128), 0)
+    lane = lax.broadcasted_iota(jnp.int32, (16, 128), 1)
+    first_cluster = morton_index() * CLUSTERS - CLUSTERS
+    listed = jnp.zeros((16, 128), jnp.int32)
+    for e in range(2):
+        owner = lax.shift_right_logical(list_ref[e, CLUSTERS - 1] * 2115, 16)
+        listed = jnp.where((row == 0) & (lane == e), owner, listed)
+        here = row == 1 + e
+        for g in range(CLUSTERS - 1):
+            listed = jnp.where(here & (lane == g), list_ref[e, g] - first_cluster, listed)
+    out_ref[OWNER_ROW : OWNER_ROW + 16, :] = listed.astype(f32).astype(bf16)
+    out = pltpu.make_async_copy(out_ref, out_hbm, out_sem.at[0])
+    out.start()
+    for copy in halves:
+        copy.wait()
+    for i in range(HALF):
+        share_ref[i] = jnp.concatenate([half_ref[i, 0], half_ref[i, 1]], axis=1)
+    share = pltpu.make_async_copy(share_ref, share_hbm, out_sem.at[1])
+    share.start()
+    out.wait()
+    share.wait()
 
 
 def up_kernel(
@@ -197,6 +226,8 @@
     copies[2].wait()
     for s in range(SLABS):
         owner_ref[s : s + 1, :] = owners_ref[s].astype(f32)[:1].astype(jnp.int32)
+    other = owners_ref[lax.axis_index("slab") ^ 1].astype(f32)
+    owner_ref[SLABS : 2 * SLABS, :] = other[:SLABS].astype(jnp.int32)
     out_rows.wait()
     out_pairs.wait()
     out_top.wait()
@@ -210,7 +241,7 @@
         (
             (tops_hbm, tops_ref),
             (matrix_hbm, matrix_ref),
-            (owner_hbm, owner_ref),
+            (owner_hbm.at[pl.ds(0, SLABS)], owner_ref),
         ),
         in_sem,
     )
@@ -226,21 +257,34 @@
         picked = jnp.concatenate([top_of(s, 0), top_of(s, 1)], axis=1)
         top = top + dot(picked, matrix_ref[s], NT)
     matrices = split(pair_matrices(transfer_ref, PAIRS - 1))
-    level = descend([dot3(split(top), matrices, NN)], transfer_ref, None)
+    level = descend([dot3(split(top), matrices, NN)], transfer_ref)
     for i in range(LEAVES // 2):
         out_ref[i] = level[i]
 
 
+def half_of(half):
+    place = 0
+    runs = []
+    for first, count in LEVELS:
+        runs.append((place, first + half * count, count))
+        place += count
+    return runs
+
+
 def field_kernel(
     list_hbm,
+    other_hbm,
     mine_hbm,
     received_hbm,
     swapped_hbm,
+    share_hbm,
     transfer_ref,
     coupling_ref,
     leaf_hbm,
     list_ref,
+    other_ref,
     window_ref,
+    share_ref,
     leaf_ref,
     in_sem,
     out_sem,
@@ -250,9 +294,14 @@
             (hbm.at[pl.ds(LEAVES, PAIRS)], window_ref.at[pl.ds(k * PAIRS, PAIRS)])
             for k, hbm in zip(window_places(), (mine_hbm, received_hbm, swapped_hbm))
         ]
-        + [(list_hbm, list_ref)],
+        + [
+            (list_hbm, list_ref),
+            (other_hbm.at[pl.ds(SLABS, SLABS)], other_ref),
+            (share_hbm, share_ref),
+        ],
         in_sem,
     )
+    half = lax.axis_index("slab") % 2
     left = lax.broadcasted_iota(jnp.int32, (RHS, 128), 1) < RANK
     first_cluster = morton_index() * CLUSTERS - CLUSTERS
     for copy in copies:
@@ -261,8 +310,7 @@
     def swapped(x):
         return jnp.concatenate([x[:, RANK:], x[:, :RANK]], axis=1)
 
-    def pick(g, e):
-        local = list_ref[e, g] - first_cluster
+    def pick(local, e):
         owner = (local >= CLUSTERS).astype(jnp.int32) + (local >= 2 * CLUSTERS).astype(
             jnp.int32
         )
@@ -273,19 +321,31 @@
         here = (cluster - 2 * pair) == e
         return jnp.where(here, high, swapped(high)), jnp.where(here, low, swapped(low))
 
-    def coupled(g):
-        matrices = split(
-            jnp.concatenate([coupling_ref[g, 0], coupling_ref[g, 1]], axis=1)
+    def pick_two(locals_of):
+        (high0, low0), (high1, low1) = pick(locals_of(0), 0), pick(locals_of(1), 1)
+        return jnp.where(left, high0, high1), jnp.where(left, low0, low1)
+
+    def coupled(place, g):
+        own = pick_two(lambda e: list_ref[e, g] - first_cluster)
+        other = pick_two(lambda e: other_ref[1 + e, g])
+        picked = [jnp.concatenate([x, y], axis=1) for x, y in zip(own, other)]
+        matrices = jnp.concatenate(
+            [coupling_ref[g, 0], coupling_ref[g, 1], share_ref[place]], axis=1
         )
-        (high0, low0), (high1, low1) = pick(g, 0), pick(g, 1)
-        picked = (jnp.where(left, high0, high1), jnp.where(left, low0, low1))
-        return dot3(picked, matrices, NT)
-
-    def own(i):
-        return jnp.concatenate([coupled(2 * i), coupled(2 * i + 1)], axis=1)
-
-    level = descend([own(PAIRS - 1)], transfer_ref, own)
-    for i in range(LEAVES // 2):
+        return dot3(picked, split(matrices), NT)
+
+    runs = half_of(half)
+    place, g, _ = runs[-1]
+    level = [coupled(place, g)]
+    for place, first, count in reversed(runs[:-1]):
+        parents, level = level, []
+        for i, parent in enumerate(parents):
+            own = [coupled(place + 2 * i + k, first + 2 * i + k) for k in range(2)]
+            pair = lax.shift_right_logical(first, 1) + i
+            passed = dot3(split(parent), split(pair_matrices(transfer_ref, pair)), NN)
+            total = jnp.concatenate(own, axis=1) + passed
+            level += [total] if count == LEAVES // 2 else [total[:, :RANK], total[:, RANK:]]
+    for i in range(LEAVES // 4):
         leaf_ref[i * RHS : (i + 1) * RHS, :] = level[i].astype(bf16)
     for copy in fetch([(leaf_ref, leaf_hbm.at[s]) for s in range(SLABS)], out_sem):
         copy.wait()
@@ -357,20 +417,13 @@
 
 
 def far_kernel(parts_hbm, extra_ref, basis_ref, near_ref, out_ref, parts_ref, sem):
-    half = LEAVES // 4 * RHS
-    copies = fetch(
-        [
-            (parts_hbm.at[:, pl.ds(k * half, half)], parts_ref.at[:, pl.ds(k * half, half)])
-            for k in range(2)
-        ],
-        sem,
-    )
+    copies = fetch([(parts_hbm, parts_ref)], sem)
+    copies[0].wait()
     for i in range(LEAVES // 2):
-        if i % (LEAVES // 4) == 0:
-            copies[i // (LEAVES // 4)].wait()
-        rows = pl.ds(i * RHS, RHS)
+        half, place = divmod(i, LEAVES // 4)
+        rows = pl.ds(place * RHS, RHS)
         total = extra_ref[i]
-        for s in range(SLABS):
+        for s in range(half, SLABS, 2):
             total = total + parts_ref[s, rows, :].astype(f32)
         high, low = split(total)
         both = jnp.concatenate([high, low], axis=0)
@@ -435,20 +488,24 @@
             **params,
         )
 
-    (packed,) = call(
+    packed, share = call(
         pack_kernel,
         "pack",
-        [((PACKED, 128), bf16)],
+        [((PACKED, 128), bf16, HBM), ((HALF, RANK, 128), f32, HBM)],
         hbm(4),
-        vmem(1),
-        [
+        hbm(2),
+        [
+            pltpu.VMEM((PACKED, 128), bf16),
+            pltpu.VMEM((HALF, RANK, 128), f32),
             pltpu.VMEM(sources.shape, bf16),
             pltpu.VMEM((LEAVES, PART, RANK), bf16),
             pltpu.VMEM(coupling.shape[1:], f32),
+            pltpu.VMEM((HALF, *coupling.shape[1:]), f32),
             pltpu.SMEM(listed.shape, jnp.int32),
             dma((4,)),
-        ],
-        limit=56,
+            dma((len(LEVELS),)),
+            dma((2,)),
+        ],
     )(
         pin(listed, HBM),
         pin(sources, HBM),
@@ -463,7 +520,7 @@
             ((LEAVES + PAIRS, RHS, POINTS), bf16, HBM),
             ((count, RHS // 2, 128), bf16, HBM),
             ((SLABS, RANK, 128), bf16, HBM),
-            ((SLABS, 128), jnp.int32),
+            ((2 * SLABS, 128), jnp.int32),
         ],
         hbm(1) + vmem(1),
         hbm(3) + vmem(1),
@@ -485,32 +542,25 @@
                 moves.append((m * SLABS + s, to * SLABS + s))
     received = lax.ppermute(mine, ("z", "y", "slab"), moves)
     swapped = lax.ppermute(received, "slab", [(s, s ^ 1) for s in range(SLABS)])
+    share = lax.ppermute(share, "slab", [(s, s ^ 1) for s in range(SLABS)])
     mine, received, swapped = pin(mine, HBM), pin(received, HBM), pin(swapped, HBM)
     tops = lax.all_to_all(top, ("z", "y"), 0, 0)
     (leaf,) = call(
         field_kernel,
         "field",
-        [
-            ((SLABS, LEAVES // 2 * RHS, 128), bf16, HBM),
-        ],
-        hbm(4) + vmem(2),
+        [((SLABS, LEAVES // 4 * RHS, 128), bf16, HBM)],
+        hbm(6) + vmem(2),
         hbm(1),
         [
             pltpu.SMEM(listed.shape, jnp.int32),
+            pltpu.SMEM((SLABS, 128), jnp.int32),
             pltpu.VMEM((3 * PAIRS, RHS, 256), bf16),
-            pltpu.VMEM((LEAVES // 2 * RHS, 128), bf16),
-            dma((4,)),
+            pltpu.VMEM((HALF, RANK, 128), f32),
+            pltpu.VMEM((LEAVES // 4 * RHS, 128), bf16),
+            dma((6,)),
             dma((SLABS,)),
         ],
-
-    )(
-        listed,
-        mine,
-        received,
-        swapped,
-        transfer,
-        coupling,
-    )
+    )(listed, owner, mine, received, swapped, pin(share, HBM), transfer, coupling)
     parts = lax.all_to_all(leaf, "slab", 0, 0)
     (near,) = call(
         near_kernel,
@@ -557,7 +607,7 @@
         [((LEAVES, RHS, PART), f32)],
         hbm(1) + vmem(3),
         vmem(1),
-        [pltpu.VMEM((SLABS, LEAVES // 2 * RHS, 128), bf16), dma((2,))],
+        [pltpu.VMEM((SLABS, LEAVES // 4 * RHS, 128), bf16), dma((1,))],
     )(parts, extra, jnp.swapaxes(basis_out, 1, 2), near)
     return out
 

time: 68.9 us -> 67.4 us (0.978)
  waiting for transfers between devices: 8.3 us -> 3.97 us
  starting transfers between devices: 23.1 us -> 25 us
    all_to_all x1, waiting for transfers between devices: 2.74 us -> 0.01 us  [shards(): parts = lax.all_to_all(leaf, 'slab', 0, 0)]
    ppermute x0 -> x1, waiting for transfers between devices: none -> 2.04 us  [shards(): share = lax.ppermute(share, 'slab', [(s, s ^ 1) for s in range(SLABS)])]
    all_to_all x1, waiting for transfers between devices: 3.85 us -> 1.92 us  [shards(): tops = lax.all_to_all(top, ('z', 'y'), 0, 0)]
    ppermute x0 -> x1, starting transfers between devices: none -> 1.92 us  [shards(): share = lax.ppermute(share, 'slab', [(s, s ^ 1) for s in range(SLABS)])]
    ppermute x1, waiting for transfers between devices: 1.7 us -> 0.01 us  [shards(): swapped = lax.ppermute(received, 'slab', [(s, s ^ 1) for s in range(SLABS)])]
  transfers between devices with their start and end apart: 4 -> 5, of which waited for: 3 -> 2; matrix products, arithmetic and copies ran while one was open for 0% -> 0% of each run, Pallas kernels for 14% -> 15%
where the time goes in v2:
time: 67.4 us; the launch traced here: 67 us
  starting transfers between devices  25 us (37%)
  blocking collectives  20.6 us (31%)
  Pallas kernels  15.5 us (23%)
  waiting for transfers between devices  3.97 us (6%)
  local copies, waits for them, and re-layouts  1.02 us (2%)
  between operations  0.82 us (1%)
    all_gather x1, blocking collectives, shards(): gathered = lax.all_gather(packed, 'slab')  20.6 us
    all_to_all x1, starting transfers between devices, shards(): tops = lax.all_to_all(top, ('z', 'y'), 0, 0)  12.2 us
    all_to_all x1, starting transfers between devices, shards(): parts = lax.all_to_all(leaf, 'slab', 0, 0)  6.87 us
    pallas_call x1, Pallas kernels, shards(): call(near_kernel, 'near', [((LEAVES, RHS, PART), f32)], hbm(8), vmem(1),...  4.66 us
    pallas_call x1, Pallas kernels, shards(): call(field_kernel, 'field', [((SLABS, LEAVES // 4 * RHS, 128), bf16, HBM)...  3.15 us
    ppermute x1, starting transfers between devices, shards(): swapped = lax.ppermute(received, 'slab', [(s, s ^ 1) for s in range(SLABS)])  2.75 us
    pallas_call x1, Pallas kernels, shards(): call(pack_kernel, 'pack', [((PACKED, 128), bf16, HBM), ((HALF, RANK, 128)...  2.55 us
    pallas_call x1, Pallas kernels, shards(): call(up_kernel, 'up', [((LEAVES + PAIRS, RHS, POINTS), bf16, HBM), ((coun...  2.23 us
  transfers between devices with their start and end apart: 5, of which 2 were waited for; matrix products, arithmetic and copies ran while one was open for 0% of the time, Pallas kernels for 15%

profile of v2, /device:TPU:1, one launch (start us, length us, event | category | flops | bytes accessed | tf_op | source)
XLA Modules:
  0.0 67.0 jit_solution(4048597310743457703)
XLA Ops:
  0.0 0.0 copy-start.1
  0.0 0.0 copy-start.4
  0.0 0.0 copy-start
  0.0 2.6 %pack.1 = (bf16[464,128]{1,0:T(8,128)(2,1)}, f32[15,64,128]{2,1,0:T(8,128)}) custom-call(s32[2,31]{1,0:T(2,128)} %bitcast.6, bf16[16,32,32]{2,1,0:T(8,128)(2,1)} %sources_hbm.1, bf16[16,32,64]{2,1,0:T(8,128)(2,1)} %bitcast.8, f32[31,2,64,64]{3,2,1,0:T(8,128)} %coupling_ref.1), custom_call_target="tpu_custom_call" | custom-call | tf_op jit(solution)/shard_map/pack/pallas_call | solution.py:491
  2.6 20.6 %all-gather = bf16[3712,128]{1,0:T(8,128)(2,1)S(1)} all-gather(bf16[464,128]{1,0:T(8,128)(2,1)} %get-tuple-element.11), channel_id=2, replica_groups=mesh['z'=8,'y'=8,'slab'=8] {'slab'}, dimensions={0}, use_global_device_ids=true | all-gather | bytes 1069056 | tf_op jit(solution)/shard_map/all_gather | solution.py:515
  23.2 0.0 copy-done
  23.2 2.2 %up.1 = (bf16[31,32,256]{2,1,0:T(8,128)(2,1)}, bf16[64,16,128]{2,1,0:T(8,128)(2,1)}, bf16[8,64,128]{2,1,0:T(8,128)(2,1)}, s32[16,128]{1,0:T(8,128)S(1)}) custom-call(bf16[8,464,128]{2,1,0:T(8,128)(2,1)S(1)} %bitcast.4, f32[30,64,64]{2,1,0:T(8,128)S(1)} %copy-done), custom_call_target="tpu_custom_call" | custom-call | tf_op jit(solution)/shard_map/up/pallas_call | solution.py:516
  25.4 1.3 %collective-permute-start = (bf16[31,32,256]{2,1,0:T(8,128)(2,1)}, bf16[31,32,256]{2,1,0:T(8,128)(2,1)}, u32[]{:S(2)}, u32[]{:S(2)}) collective-permute-start(bf16[31,32,256]{2,1,0:T(8,128)(2,1)} %get-tuple-element.13.mine_hbm), channel_id=1, source_target_pairs={{0,8},{2,10},{4,12},{6,14},{8,16},{9,1},{10,18},{11,3},{12,20},{13... | collective-permute-start | bytes 1523720 | tf_op jit(solution)/shard_map/ppermute | solution.py:543
  26.7 0.0 copy-start.2
  26.7 12.2 %all-to-all-start.1 = ((bf16[64,16,128]{2,1,0:T(8,128)(2,1)}), bf16[64,16,128]{2,1,0:T(8,128)(2,1)S(1)}, u32[]{:S(2)}, u32[]{:S(2)}) async-start(bf16[64,16,128]{2,1,0:T(8,128)(2,1)} %get-tuple-element.15), calls=%async_computation.1 | async-start | bytes 524288 | tf_op jit(solution)/shard_map/all_to_all | solution.py:547
  38.9 0.0 collective-permute-done.received_hbm
  38.9 2.7 %collective-permute-start.1 = (bf16[31,32,256]{2,1,0:T(8,128)(2,1)}, bf16[31,32,256]{2,1,0:T(8,128)(2,1)S(1)}, u32[]{:S(2)}, u32[]{:S(2)}) collective-permute-start(bf16[31,32,256]{2,1,0:T(8,128)(2,1)} %collective-permute-done.received_hbm), channel_id=1, source_target_pairs={{0,1},{1,0},{2,3},{3,2},{4,5},{5,4},{6,7},{7,6},{8,9},{9,8},{10,11... | collective-permute-start | bytes 1523720 | tf_op jit(solution)/shard_map/ppermute | solution.py:544
  41.7 1.9 %collective-permute-start.2 = (f32[15,64,128]{2,1,0:T(8,128)}, f32[15,64,128]{2,1,0:T(8,128)S(1)}, u32[]{:S(2)}, u32[]{:S(2)}) collective-permute-start(f32[15,64,128]{2,1,0:T(8,128)} %get-tuple-element.14), channel_id=1, source_target_pairs={{0,1},{1,0},{2,3},{3,2},{4,5},{5,4},{6,7},{7,6},{8,9},{9,8},{10,11... | collective-permute-start | bytes 1474568 | tf_op jit(solution)/shard_map/ppermute | solution.py:545
  43.6 2.0 %collective-permute-done.2.share_hbm = f32[15,64,128]{2,1,0:T(8,128)S(1)} collective-permute-done((f32[15,64,128]{2,1,0:T(8,128)}, f32[15,64,128]{2,1,0:T(8,128)S(1)}, u32[]{:S(2)}, u32[]{:S(2)}) %collective-permute-start.2) | collective-permute-done | bytes 491552 | tf_op jit(solution)/shard_map/ppermute | solution.py:545
  45.7 0.0 copy-start.9
  45.7 0.0 collective-permute-done.1.swapped_hbm
  45.7 0.0 copy-start.8
  45.7 0.8 %copy-done.9 = f32[15,64,128]{2,1,0:T(8,128)} copy-done((f32[15,64,128]{2,1,0:T(8,128)}, f32[15,64,128]{2,1,0:T(8,128)S(1)}, u32[]{:S(2)}) %copy-start.9) | copy-done | bytes 491544
  46.5 0.2 copy-done.8
  46.7 0.0 copy-done.1
  46.7 0.0 copy-done.4
  46.7 0.0 copy-start.5
  46.7 0.0 copy-start.6
  46.7 0.0 copy-start.7
  46.7 3.1 %field.1 = bf16[8,128,128]{2,1,0:T(8,128)(2,1)} custom-call(s32[2,31]{1,0:T(2,128)S(1)} %bitcast.7, s32[16,128]{1,0:T(8,128)S(1)} %get-tuple-element.12.other_hbm.owner_hbm, bf16[31,32,256]{2,1,0:T(8,128)(2,1)} %get-tuple-element.13.mine_hbm, bf16[31,32,256]{2,1,0:T(8,128)(2,1)} %collective-permute-done.received_hbm, bf16[31,32,256]{2,1,0:T(8,128)(2,1)} %copy-done.8, ...), custom_call_target="tpu_custom_call" | custom-call | tf_op jit(solution)/shard_map/field/pallas_call | solution.py:548
  49.8 1.9 %all-to-all-done.1.tops_hbm = bf16[64,16,128]{2,1,0:T(8,128)(2,1)S(1)} async-done(((bf16[64,16,128]{2,1,0:T(8,128)(2,1)}), bf16[64,16,128]{2,1,0:T(8,128)(2,1)S(1)}, u32[]{:S(2)}, u32[]{:S(2)}) %all-to-all-start.1) | async-done | bytes 262176 | tf_op jit(solution)/shard_map/all_to_all | solution.py:547
  51.8 6.9 %all-to-all-start = ((bf16[8,128,128]{2,1,0:T(8,128)(2,1)}), bf16[8,128,128]{2,1,0:T(8,128)(2,1)S(1)}, u32[]{:S(2)}, u32[]{:S(2)}) async-start(bf16[8,128,128]{2,1,0:T(8,128)(2,1)} %field.1), calls=%async_computation | async-start | bytes 524288 | tf_op jit(solution)/shard_map/all_to_all | solution.py:564
  59.3 0.0 copy-done.2
  59.3 0.0 copy-start.3
  59.3 1.9 %top.1.extra_ref = f32[8,32,128]{2,1,0:T(8,128)S(1)} custom-call(s32[16,128]{1,0:T(8,128)S(1)} %get-tuple-element.12.other_hbm.owner_hbm, bf16[64,16,128]{2,1,0:T(8,128)(2,1)S(1)} %all-to-all-done.1.tops_hbm, bf16[8,64,128]{2,1,0:T(8,128)(2,1)S(1)} %copy-done.2, f32[30,64,64]{2,1,0:T(8,128)S(1)} %copy-done), custom_call_target="tpu_custom_call" | custom-call | tf_op jit(solution)/shard_map/top/pallas_call | solution.py:591
  61.2 0.0 copy-done.5
  61.2 0.0 copy-done.6
  61.3 0.0 copy-done.7
  61.3 4.7 %near.1.near_ref = f32[16,32,32]{2,1,0:T(8,128)S(1)} custom-call(f32[192]{0:T(256)S(1)} %copy-done.5, s32[192]{0:T(256)S(1)} %copy-done.6, s32[192]{0:T(256)S(1)} %copy-done.7, s32[1]{0:T(128)S(6)} %copy.12.count_hbm, bf16[31,32,256]{2,1,0:T(8,128)(2,1)} %get-tuple-element.13.mine_hbm, bf16[31,32,256]{2,1,0:T(8,128)(2,1)} %collective-permute-done.received_hbm, ...), custom_call_target="tpu_custom_call" | custom-call | tf_op jit(solution)/shard_map/near/pallas_call | solution.py:565
  65.9 0.0 all-to-all-done.parts_hbm
  66.0 0.0 copy-done.3
  66.0 1.0 %far.1 = f32[16,32,32]{2,1,0:T(8,128)} custom-call(bf16[8,128,128]{2,1,0:T(8,128)(2,1)S(1)} %all-to-all-done.parts_hbm, f32[8,32,128]{2,1,0:T(8,128)S(1)} %top.1.extra_ref, bf16[16,32,64]{2,1,0:T(8,128)(2,1)S(1)} %bitcast.5, f32[16,32,32]{2,1,0:T(8,128)S(1)} %near.1.near_ref), custom_call_target="tpu_custom_call" | custom-call | tf_op jit(solution)/shard_map/far/pallas_call | solution.py:604
Async XLA Ops:
  0.0 46.7 %copy-start.1 = (f32[31,2,64,64]{3,2,1,0:T(8,128)S(1)}, f32[31,2,64,64]{3,2,1,0:T(8,128)}, u32[]{:S(2)}) copy-start(f32[31,2,64,64]{3,2,1,0:T(8,128)} %coupling_ref.1) | copy-start | bytes 3047428
  0.0 46.7 %copy-start.4 = (s32[31,2]{0,1:T(2,128)S(1)}, s32[31,2]{0,1:T(2,128)}, u32[]{:S(2)}) copy-start(s32[31,2]{0,1:T(2,128)} %param.16) | copy-start | bytes 748
  0.0 23.2 %copy-start = (f32[30,64,64]{2,1,0:T(8,128)S(1)}, f32[30,64,64]{2,1,0:T(8,128)}, u32[]{:S(2)}) copy-start(f32[30,64,64]{2,1,0:T(8,128)} %transfer_ref.5) | copy-start | bytes 1474564
  25.4 13.5 %collective-permute-start = (bf16[31,32,256]{2,1,0:T(8,128)(2,1)}, bf16[31,32,256]{2,1,0:T(8,128)(2,1)}, u32[]{:S(2)}, u32[]{:S(2)}) collective-permute-start(bf16[31,32,256]{2,1,0:T(8,128)(2,1)} %get-tuple-element.13.mine_hbm), channel_id=1, source_target_pairs={{0,8},{2,10},{4,12},{6,14},{8,16},{9,1},{10,18},{11,3},{12,20},{13... | collective-permute-start | bytes 1523720 | tf_op jit(solution)/shard_map/ppermute | solution.py:543
  26.7 32.6 %copy-start.2 = (bf16[8,64,128]{2,1,0:T(8,128)(2,1)S(1)}, bf16[8,64,128]{2,1,0:T(8,128)(2,1)}, u32[]{:S(2)}) copy-start(bf16[8,64,128]{2,1,0:T(8,128)(2,1)} %get-tuple-element.16.matrix_hbm) | copy-start | bytes 393220
  26.7 25.0 %all-to-all-start.1 = ((bf16[64,16,128]{2,1,0:T(8,128)(2,1)}), bf16[64,16,128]{2,1,0:T(8,128)(2,1)S(1)}, u32[]{:S(2)}, u32[]{:S(2)}) async-start(bf16[64,16,128]{2,1,0:T(8,128)(2,1)} %get-tuple-element.15), calls=%async_computation.1 | async-start | bytes 524288 | tf_op jit(solution)/shard_map/all_to_all | solution.py:547
  38.9 6.7 %collective-permute-start.1 = (bf16[31,32,256]{2,1,0:T(8,128)(2,1)}, bf16[31,32,256]{2,1,0:T(8,128)(2,1)S(1)}, u32[]{:S(2)}, u32[]{:S(2)}) collective-permute-start(bf16[31,32,256]{2,1,0:T(8,128)(2,1)} %collective-permute-done.received_hbm), channel_id=1, source_target_pairs={{0,1},{1,0},{2,3},{3,2},{4,5},{5,4},{6,7},{7,6},{8,9},{9,8},{10,11... | collective-permute-start | bytes 1523720 | tf_op jit(solution)/shard_map/ppermute | solution.py:544
  41.7 4.0 %collective-permute-start.2 = (f32[15,64,128]{2,1,0:T(8,128)}, f32[15,64,128]{2,1,0:T(8,128)S(1)}, u32[]{:S(2)}, u32[]{:S(2)}) collective-permute-start(f32[15,64,128]{2,1,0:T(8,128)} %get-tuple-element.14), channel_id=1, source_target_pairs={{0,1},{1,0},{2,3},{3,2},{4,5},{5,4},{6,7},{7,6},{8,9},{9,8},{10,11... | collective-permute-start | bytes 1474568 | tf_op jit(solution)/shard_map/ppermute | solution.py:545
  45.7 0.8 %copy-start.9 = (f32[15,64,128]{2,1,0:T(8,128)}, f32[15,64,128]{2,1,0:T(8,128)S(1)}, u32[]{:S(2)}) copy-start(f32[15,64,128]{2,1,0:T(8,128)S(1)} %collective-permute-done.2.share_hbm) | copy-start | bytes 1474564
  45.7 1.0 %copy-start.8 = (bf16[31,32,256]{2,1,0:T(8,128)(2,1)}, bf16[31,32,256]{2,1,0:T(8,128)(2,1)S(1)}, u32[]{:S(2)}) copy-start(bf16[31,32,256]{2,1,0:T(8,128)(2,1)S(1)} %collective-permute-done.1.swapped_hbm) | copy-start | bytes 1523716
  46.7 14.6 %copy-start.5 = (f32[192]{0:T(256)S(1)}, f32[192]{0:T(256)}, u32[]{:S(2)}) copy-start(f32[192]{0:T(256)} %scale_hbm.1) | copy-start | bytes 2308
  46.7 14.6 %copy-start.6 = (s32[192]{0:T(256)S(1)}, s32[192]{0:T(256)}, u32[]{:S(2)}) copy-start(s32[192]{0:T(256)} %target_hbm.1) | copy-start | bytes 2308
  46.7 14.6 %copy-start.7 = (s32[192]{0:T(256)S(1)}, s32[192]{0:T(256)}, u32[]{:S(2)}) copy-start(s32[192]{0:T(256)} %source_hbm.1) | copy-start | bytes 2308
  51.8 14.2 %all-to-all-start = ((bf16[8,128,128]{2,1,0:T(8,128)(2,1)}), bf16[8,128,128]{2,1,0:T(8,128)(2,1)S(1)}, u32[]{:S(2)}, u32[]{:S(2)}) async-start(bf16[8,128,128]{2,1,0:T(8,128)(2,1)} %field.1), calls=%async_computation | async-start | bytes 524288 | tf_op jit(solution)/shard_map/all_to_all | solution.py:564
  59.3 6.7 %copy-start.3 = (bf16[16,64,32]{1,2,0:T(8,128)(2,1)S(1)}, bf16[16,64,32]{1,2,0:T(8,128)(2,1)}, u32[]{:S(2)}) copy-start(bf16[16,64,32]{1,2,0:T(8,128)(2,1)} %param.13) | copy-start | bytes 196612

commit v3 on v2

--- a/solution.py
+++ b/solution.py
@@ -20,7 +20,7 @@
 TOP_ROW = SRC_ROWS + BASIS_ROWS
 OWNER_ROW = TOP_ROW + RANK
 PACKED = OWNER_ROW + 16
-TILE_SLOTS = 8
+TILE_SLOTS = 48
 NEAR_CHUNKS = 4
 bf16 = jnp.bfloat16
 f32 = jnp.float32
@@ -171,32 +171,22 @@
 
 
 def up_kernel(
-    packed_hbm,
+    packed_ref,
     transfer_ref,
     mine_hbm,
     top_hbm,
     matrix_hbm,
     owner_ref,
-    sources_ref,
-    basis_ref,
-    owners_ref,
     mine_ref,
     top_ref,
-    in_sem,
     out_sem,
 ):
-    copies = fetch(
-        (
-            (packed_hbm.at[:, pl.ds(0, SRC_ROWS)], sources_ref),
-            (packed_hbm.at[:, pl.ds(SRC_ROWS, BASIS_ROWS)], basis_ref),
-            (packed_hbm.at[:, pl.ds(OWNER_ROW, 16)], owners_ref),
-            (packed_hbm.at[:, pl.ds(TOP_ROW, RANK)], matrix_hbm),
-        ),
-        in_sem,
-    )
-    copies[0].wait()
+    out_matrix = pltpu.make_async_copy(
+        packed_ref.at[:, pl.ds(TOP_ROW, RANK)], matrix_hbm, out_sem.at[3]
+    )
+    out_matrix.start()
     for g in range(LEAVES // 4):
-        tiles = [sources_ref[s, g * RHS : (g + 1) * RHS, :] for s in range(SLABS)]
+        tiles = [packed_ref[s, g * RHS : (g + 1) * RHS, :] for s in range(SLABS)]
         for i in range(4):
             mine_ref[4 * g + i] = jnp.concatenate(
                 [t[:, i * PART : (i + 1) * PART] for t in tiles], axis=1
@@ -204,11 +194,11 @@
     rows = pl.ds(0, LEAVES)
     out_rows = pltpu.make_async_copy(mine_ref.at[rows], mine_hbm.at[rows], out_sem.at[0])
     out_rows.start()
-    copies[1].wait()
     pairs = []
     for i in range(LEAVES // 2):
+        start = SRC_ROWS + i * PART
         basis = jnp.concatenate(
-            [basis_ref[s, i * PART : (i + 1) * PART, :] for s in range(SLABS)], axis=0
+            [packed_ref[s, start : start + PART, :] for s in range(SLABS)], axis=0
         )
         pairs.append(leaf_pair([mine_ref[2 * i], mine_ref[2 * i + 1]], basis))
 
@@ -223,43 +213,14 @@
     top_ref[...] = jnp.broadcast_to(row[None], top_ref.shape)
     out_top = pltpu.make_async_copy(top_ref, top_hbm, out_sem.at[2])
     out_top.start()
-    copies[2].wait()
     for s in range(SLABS):
-        owner_ref[s : s + 1, :] = owners_ref[s].astype(f32)[:1].astype(jnp.int32)
-    other = owners_ref[lax.axis_index("slab") ^ 1].astype(f32)
+        owner_ref[s : s + 1, :] = packed_ref[s, OWNER_ROW:].astype(f32)[:1].astype(jnp.int32)
+    other = packed_ref[lax.axis_index("slab") ^ 1, OWNER_ROW:].astype(f32)
     owner_ref[SLABS : 2 * SLABS, :] = other[:SLABS].astype(jnp.int32)
     out_rows.wait()
     out_pairs.wait()
     out_top.wait()
-    copies[3].wait()
-
-
-def top_kernel(
-    owner_hbm, tops_hbm, matrix_hbm, transfer_ref, out_ref, owner_ref, tops_ref, matrix_ref, in_sem
-):
-    copies = fetch(
-        (
-            (tops_hbm, tops_ref),
-            (matrix_hbm, matrix_ref),
-            (owner_hbm.at[pl.ds(0, SLABS)], owner_ref),
-        ),
-        in_sem,
-    )
-    for copy in copies:
-        copy.wait()
-
-    def top_of(s, e):
-        block = tops_ref[owner_ref[s, e]]
-        return jnp.concatenate([block[:, :RANK], block[:, RANK:]], axis=0)
-
-    top = jnp.zeros((RHS, RANK), f32)
-    for s in range(SLABS):
-        picked = jnp.concatenate([top_of(s, 0), top_of(s, 1)], axis=1)
-        top = top + dot(picked, matrix_ref[s], NT)
-    matrices = split(pair_matrices(transfer_ref, PAIRS - 1))
-    level = descend([dot3(split(top), matrices, NN)], transfer_ref)
-    for i in range(LEAVES // 2):
-        out_ref[i] = level[i]
+    out_matrix.wait()
 
 
 def half_of(half):
@@ -277,16 +238,30 @@
     mine_hbm,
     received_hbm,
     swapped_hbm,
-    share_hbm,
+    scale_hbm,
+    target_hbm,
+    source_hbm,
+    count_hbm,
+    near_hbm,
+    share_ref,
     transfer_ref,
     coupling_ref,
     leaf_hbm,
+    out_ref,
     list_ref,
     other_ref,
     window_ref,
-    share_ref,
+    high_ref,
+    low_ref,
     leaf_ref,
+    scale_ref,
+    target_ref,
+    source_ref,
+    count_ref,
+    rows_ref,
+    near_ref,
     in_sem,
+    near_sem,
     out_sem,
 ):
     copies = fetch(
@@ -297,11 +272,36 @@
         + [
             (list_hbm, list_ref),
             (other_hbm.at[pl.ds(SLABS, SLABS)], other_ref),
-            (share_hbm, share_ref),
         ],
         in_sem,
     )
-    half = lax.axis_index("slab") % 2
+    chunk = near_ref.shape[0] // NEAR_CHUNKS
+    near_copies = fetch(
+        [
+            (scale_hbm, scale_ref),
+            (target_hbm, target_ref),
+            (source_hbm, source_ref),
+            (count_hbm, count_ref),
+        ]
+        + [
+            (hbm.at[pl.ds(0, LEAVES)], rows_ref.at[pl.ds(k * LEAVES, LEAVES)])
+            for k, hbm in zip(window_places(), (mine_hbm, received_hbm, swapped_hbm))
+        ]
+        + [
+            (near_hbm.at[pl.ds(k * chunk, chunk)], near_ref.at[pl.ds(k * chunk, chunk)])
+            for k in range(NEAR_CHUNKS)
+        ],
+        near_sem,
+    )
+    out_ref[...] = jnp.zeros_like(out_ref)
+    runs = half_of(lax.axis_index("slab") % 2)
+    for start, first, count in runs:
+        for i in range(count):
+            matrices = jnp.concatenate(
+                [coupling_ref[first + i, 0], coupling_ref[first + i, 1], share_ref[start + i]],
+                axis=1,
+            )
+            high_ref[start + i], low_ref[start + i] = split(matrices)
     left = lax.broadcasted_iota(jnp.int32, (RHS, 128), 1) < RANK
     first_cluster = morton_index() * CLUSTERS - CLUSTERS
     for copy in copies:
@@ -329,12 +329,8 @@
         own = pick_two(lambda e: list_ref[e, g] - first_cluster)
         other = pick_two(lambda e: other_ref[1 + e, g])
         picked = [jnp.concatenate([x, y], axis=1) for x, y in zip(own, other)]
-        matrices = jnp.concatenate(
-            [coupling_ref[g, 0], coupling_ref[g, 1], share_ref[place]], axis=1
-        )
-        return dot3(picked, split(matrices), NT)
-
-    runs = half_of(half)
+        return dot3(picked, (high_ref[place], low_ref[place]), NT)
+
     place, g, _ = runs[-1]
     level = [coupled(place, g)]
     for place, first, count in reversed(runs[:-1]):
@@ -347,78 +343,75 @@
             level += [total] if count == LEAVES // 2 else [total[:, :RANK], total[:, RANK:]]
     for i in range(LEAVES // 4):
         leaf_ref[i * RHS : (i + 1) * RHS, :] = level[i].astype(bf16)
-    for copy in fetch([(leaf_ref, leaf_hbm.at[s]) for s in range(SLABS)], out_sem):
-        copy.wait()
-
-
-def near_kernel(
-    scale_hbm,
-    target_hbm,
-    source_hbm,
-    count_hbm,
-    mine_hbm,
-    received_hbm,
-    swapped_hbm,
-    near_hbm,
-    out_ref,
-    scale_ref,
-    target_ref,
-    source_ref,
-    count_ref,
-    window_ref,
-    near_ref,
-    product_ref,
-    in_sem,
-):
-    chunk = near_ref.shape[0] // NEAR_CHUNKS
-    copies = fetch(
-        [
-            (scale_hbm, scale_ref),
-            (target_hbm, target_ref),
-            (source_hbm, source_ref),
-            (count_hbm, count_ref),
-        ]
-        + [
-            (hbm.at[pl.ds(0, LEAVES)], window_ref.at[pl.ds(k * LEAVES, LEAVES)])
-            for k, hbm in zip(window_places(), (mine_hbm, received_hbm, swapped_hbm))
-        ]
-        + [
-            (near_hbm.at[pl.ds(k * chunk, chunk)], near_ref.at[pl.ds(k * chunk, chunk)])
-            for k in range(NEAR_CHUNKS)
-        ],
-        in_sem,
-    )
-    out_ref[...] = jnp.zeros_like(out_ref)
+    leaf_copies = fetch([(leaf_ref, leaf_hbm.at[s]) for s in range(SLABS)], out_sem)
+
     morton = morton_index()
     first_source = (morton - 1) * LEAVES
     first_target = morton * LEAVES
-    for copy in copies[:-NEAR_CHUNKS]:
+    for copy in near_copies[:-NEAR_CHUNKS]:
         copy.wait()
     live = count_ref[0]
 
     def tile(t, carry):
         base = t * TILE_SLOTS
+        products = []
         for k in range(TILE_SLOTS):
             slot = base + k
             row = source_ref[slot] - first_source
-            product_ref[k] = dot(window_ref[row], near_ref[slot], NT)
+            products.append(dot(rows_ref[row], near_ref[slot], NT))
         for k in range(TILE_SLOTS):
             slot = base + k
             target = target_ref[slot] - first_target
             weight = jnp.where(slot < live, scale_ref[slot], 0.0)
-            out_ref[target] += weight * product_ref[k]
+            out_ref[target] += weight * products[k]
         return carry
 
     tiles = (live + TILE_SLOTS - 1) // TILE_SLOTS
     step = chunk // TILE_SLOTS
     for k in range(NEAR_CHUNKS):
-        copies[k - NEAR_CHUNKS].wait()
+        near_copies[k - NEAR_CHUNKS].wait()
         lax.fori_loop(k * step, jnp.clip(tiles, k * step, (k + 1) * step), tile, 0)
-
-
-def far_kernel(parts_hbm, extra_ref, basis_ref, near_ref, out_ref, parts_ref, sem):
-    copies = fetch([(parts_hbm, parts_ref)], sem)
-    copies[0].wait()
+    for copy in leaf_copies:
+        copy.wait()
+
+
+def top_kernel(
+    owner_hbm,
+    tops_hbm,
+    matrix_hbm,
+    transfer_ref,
+    extra_ref,
+    owner_ref,
+    tops_ref,
+    matrix_ref,
+    in_sem,
+):
+    copies = fetch(
+        (
+            (owner_hbm.at[pl.ds(0, SLABS)], owner_ref),
+            (tops_hbm, tops_ref),
+            (matrix_hbm, matrix_ref),
+        ),
+        in_sem,
+    )
+    for copy in copies:
+        copy.wait()
+
+    def top_of(s, e):
+        block = tops_ref[owner_ref[s, e]]
+        return jnp.concatenate([block[:, :RANK], block[:, RANK:]], axis=0)
+
+    top = jnp.zeros((RHS, RANK), f32)
+    for s in range(SLABS):
+        picked = jnp.concatenate([top_of(s, 0), top_of(s, 1)], axis=1)
+        top = top + dot(picked, matrix_ref[s], NT)
+    matrices = split(pair_matrices(transfer_ref, PAIRS - 1))
+    level = descend([dot3(split(top), matrices, NN)], transfer_ref)
+    for i in range(LEAVES // 2):
+        extra_ref[i] = level[i]
+
+
+def far_kernel(parts_ref, extra_ref, basis_ref, near_ref, out_ref):
     for i in range(LEAVES // 2):
         half, place = divmod(i, LEAVES // 4)
         rows = pl.ds(place * RHS, RHS)
@@ -522,18 +515,14 @@
             ((SLABS, RANK, 128), bf16, HBM),
             ((2 * SLABS, 128), jnp.int32),
         ],
-        hbm(1) + vmem(1),
+        vmem(2),
         hbm(3) + vmem(1),
         [
-            pltpu.VMEM((SLABS, SRC_ROWS, 128), bf16),
-            pltpu.VMEM((SLABS, BASIS_ROWS, 128), bf16),
-            pltpu.VMEM((SLABS, 16, 128), bf16),
             pltpu.VMEM((LEAVES + PAIRS, RHS, POINTS), bf16),
             pltpu.VMEM((count, RHS // 2, 128), bf16),
             dma((4,)),
-            dma((3,)),
-        ],
-    )(gathered, transfer)
+        ],
+    )(pin(gathered, pltpu.VMEM), transfer)
     moves = []
     for m in range(count):
         for s in range(SLABS):
@@ -543,51 +532,47 @@
     received = lax.ppermute(mine, ("z", "y", "slab"), moves)
     swapped = lax.ppermute(received, "slab", [(s, s ^ 1) for s in range(SLABS)])
     share = lax.ppermute(share, "slab", [(s, s ^ 1) for s in range(SLABS)])
-    mine, received, swapped = pin(mine, HBM), pin(received, HBM), pin(swapped, HBM)
+    mine, received, swapped = pin(mine, HBM), pin(received, HBM), pin(swapped, pltpu.VMEM)
     tops = lax.all_to_all(top, ("z", "y"), 0, 0)
-    (leaf,) = call(
+    leaf, near = call(
         field_kernel,
         "field",
-        [((SLABS, LEAVES // 4 * RHS, 128), bf16, HBM)],
-        hbm(6) + vmem(2),
-        hbm(1),
+        [((SLABS, LEAVES // 4 * RHS, 128), bf16, HBM), ((LEAVES, RHS, PART), f32)],
+        hbm(10) + vmem(3),
+        hbm(1) + vmem(1),
         [
             pltpu.SMEM(listed.shape, jnp.int32),
             pltpu.SMEM((SLABS, 128), jnp.int32),
             pltpu.VMEM((3 * PAIRS, RHS, 256), bf16),
-            pltpu.VMEM((HALF, RANK, 128), f32),
+            pltpu.VMEM((HALF, RANK, 256), bf16),
+            pltpu.VMEM((HALF, RANK, 256), bf16),
             pltpu.VMEM((LEAVES // 4 * RHS, 128), bf16),
-            dma((6,)),
-            dma((SLABS,)),
-        ],
-    )(listed, owner, mine, received, swapped, pin(share, HBM), transfer, coupling)
-    parts = lax.all_to_all(leaf, "slab", 0, 0)
-    (near,) = call(
-        near_kernel,
-        "near",
-        [((LEAVES, RHS, PART), f32)],
-        hbm(8),
-        vmem(1),
-        [
             pltpu.SMEM((slots,), f32),
             pltpu.SMEM((slots,), jnp.int32),
             pltpu.SMEM((slots,), jnp.int32),
             pltpu.SMEM((1,), jnp.int32),
             pltpu.VMEM((3 * LEAVES, RHS, POINTS), bf16),
             pltpu.VMEM((slots, PART, POINTS), bf16),
-            pltpu.VMEM((TILE_SLOTS, RHS, PART), f32),
+            dma((5,)),
             dma((7 + NEAR_CHUNKS,)),
+            dma((SLABS,)),
         ],
     )(
-        near_scale,
-        near_target,
-        near_source,
-        near_count,
+        listed,
+        owner,
         mine,
         received,
         swapped,
+        pin(near_scale, HBM),
+        pin(near_target, HBM),
+        pin(near_source, HBM),
+        near_count,
         pin(near_block, HBM),
-    )
+        pin(share, pltpu.VMEM),
+        transfer,
+        coupling,
+    )
+    parts = lax.all_to_all(leaf, "slab", 0, 0)
     (extra,) = call(
         top_kernel,
         "top",
@@ -600,15 +585,15 @@
             pltpu.VMEM((SLABS, RANK, 128), bf16),
             dma((3,)),
         ],
-    )(owner, tops, matrix, transfer)
+    )(pin(owner, HBM), pin(tops, HBM), pin(matrix, HBM), transfer)
     (out,) = call(
         far_kernel,
         "far",
         [((LEAVES, RHS, PART), f32)],
-        hbm(1) + vmem(3),
+        vmem(4),
         vmem(1),
-        [pltpu.VMEM((SLABS, LEAVES // 4 * RHS, 128), bf16), dma((1,))],
-    )(parts, extra, jnp.swapaxes(basis_out, 1, 2), near)
+        [],
+    )(pin(parts, pltpu.VMEM), extra, jnp.swapaxes(basis_out, 1, 2), near)
     return out
 
 

time: 67.4 us -> 66.4 us (0.985)
  Pallas kernels: 15.5 us -> 11.1 us
  waiting for transfers between devices: 3.97 us -> 8.14 us
  local copies, waits for them, and re-layouts: 1.02 us -> 0.03 us
    pallas_call x2 -> x1, Pallas kernels: 5.68 us -> 0.99 us  [shards(): call(far_kernel, 'far', [((LEAVES, RHS, PART), f32)], vmem(4), vmem(1), [])]
    all_to_all x1, waiting for transfers between devices: 0.01 us -> 4.38 us  [shards(): parts = lax.all_to_all(leaf, 'slab', 0, 0)]
    unnamed x20 -> x12, local copies, waits for them, and re-layouts: 1.02 us -> 0.03 us
    ppermute x1, waiting for transfers between devices: 2.04 us -> 1.18 us  [shards(): share = lax.ppermute(share, 'slab', [(s, s ^ 1) for s in range(SLABS)])]
  transfers between devices with their start and end apart: 5 -> 5, of which waited for: 2 -> 3; matrix products, arithmetic and copies ran while one was open for 0% -> 0% of each run, Pallas kernels for 15% -> 9%
where the time goes in v3:
time: 66.4 us; the launch traced here: 66 us
  starting transfers between devices  25.2 us (38%)
  blocking collectives  20.7 us (31%)
  Pallas kernels  11.1 us (17%)
  waiting for transfers between devices  8.14 us (12%)
  between operations  0.77 us (1%)
    all_gather x1, blocking collectives, shards(): gathered = lax.all_gather(packed, 'slab')  20.7 us
    all_to_all x1, starting transfers between devices, shards(): tops = lax.all_to_all(top, ('z', 'y'), 0, 0)  12.3 us
    all_to_all x1, starting transfers between devices, shards(): parts = lax.all_to_all(leaf, 'slab', 0, 0)  6.87 us
    all_to_all x1, waiting for transfers between devices, shards(): parts = lax.all_to_all(leaf, 'slab', 0, 0)  4.38 us
    pallas_call x1, Pallas kernels, shards(): call(field_kernel, 'field', [((SLABS, LEAVES // 4 * RHS, 128), bf16, HBM)...  3.53 us
    ppermute x1, starting transfers between devices, shards(): swapped = lax.ppermute(received, 'slab', [(s, s ^ 1) for s in range(SLABS)])  2.75 us
    all_to_all x1, waiting for transfers between devices, shards(): tops = lax.all_to_all(top, ('z', 'y'), 0, 0)  2.57 us
    pallas_call x1, Pallas kernels, shards(): call(pack_kernel, 'pack', [((PACKED, 128), bf16, HBM), ((HALF, RANK, 128)...  2.54 us
  transfers between devices with their start and end apart: 5, of which 3 were waited for; matrix products, arithmetic and copies ran while one was open for 0% of the time, Pallas kernels for 9%

profile of v3, /device:TPU:1, one launch (start us, length us, event | category | flops | bytes accessed | tf_op | source)
XLA Modules:
  0.0 66.0 jit_solution(2740823820652503325)
XLA Ops:
  0.0 0.0 copy-start.1
  0.0 0.0 copy-start.4
  0.0 0.0 copy-start
  0.0 2.5 %pack.1 = (bf16[464,128]{1,0:T(8,128)(2,1)}, f32[15,64,128]{2,1,0:T(8,128)}) custom-call(s32[2,31]{1,0:T(2,128)} %bitcast.6, bf16[16,32,32]{2,1,0:T(8,128)(2,1)} %sources_hbm.1, bf16[16,32,64]{2,1,0:T(8,128)(2,1)} %bitcast.8, f32[31,2,64,64]{3,2,1,0:T(8,128)} %coupling_ref.1), custom_call_target="tpu_custom_call" | custom-call | tf_op jit(solution)/shard_map/pack/pallas_call | solution.py:484
  2.6 0.0 copy-start.5
  2.6 20.7 %all-gather = bf16[3712,128]{1,0:T(8,128)(2,1)S(1)} all-gather(bf16[464,128]{1,0:T(8,128)(2,1)} %get-tuple-element.13), channel_id=2, replica_groups=mesh['z'=8,'y'=8,'slab'=8] {'slab'}, dimensions={0}, use_global_device_ids=true | all-gather | bytes 1069056 | tf_op jit(solution)/shard_map/all_gather | solution.py:508
  23.3 0.0 copy-done
  23.3 2.0 %up.1 = (bf16[31,32,256]{2,1,0:T(8,128)(2,1)}, bf16[64,16,128]{2,1,0:T(8,128)(2,1)}, bf16[8,64,128]{2,1,0:T(8,128)(2,1)}, s32[16,128]{1,0:T(8,128)S(1)}) custom-call(bf16[8,464,128]{2,1,0:T(8,128)(2,1)S(1)} %bitcast.4, f32[30,64,64]{2,1,0:T(8,128)S(1)} %copy-done), custom_call_target="tpu_custom_call" | custom-call | tf_op jit(solution)/shard_map/up/pallas_call | solution.py:509
  25.3 0.0 copy-start.3
  25.3 1.3 %collective-permute-start = (bf16[31,32,256]{2,1,0:T(8,128)(2,1)}, bf16[31,32,256]{2,1,0:T(8,128)(2,1)}, u32[]{:S(2)}, u32[]{:S(2)}) collective-permute-start(bf16[31,32,256]{2,1,0:T(8,128)(2,1)} %get-tuple-element.15.mine_hbm), channel_id=1, source_target_pairs={{0,8},{2,10},{4,12},{6,14},{8,16},{9,1},{10,18},{11,3},{12,20},{13... | collective-permute-start | bytes 1523720 | tf_op jit(solution)/shard_map/ppermute | solution.py:532
  26.6 12.3 %all-to-all-start.1 = ((bf16[64,16,128]{2,1,0:T(8,128)(2,1)}), bf16[64,16,128]{2,1,0:T(8,128)(2,1)}, u32[]{:S(2)}, u32[]{:S(2)}) async-start(bf16[64,16,128]{2,1,0:T(8,128)(2,1)} %get-tuple-element.18), calls=%async_computation.1 | async-start | bytes 524288 | tf_op jit(solution)/shard_map/all_to_all | solution.py:536
  38.9 0.0 collective-permute-done.received_hbm
  38.9 2.7 %collective-permute-start.1 = (bf16[31,32,256]{2,1,0:T(8,128)(2,1)}, bf16[31,32,256]{2,1,0:T(8,128)(2,1)S(1)}, u32[]{:S(2)}, u32[]{:S(2)}) collective-permute-start(bf16[31,32,256]{2,1,0:T(8,128)(2,1)} %collective-permute-done.received_hbm), channel_id=1, source_target_pairs={{0,1},{1,0},{2,3},{3,2},{4,5},{5,4},{6,7},{7,6},{8,9},{9,8},{10,11... | collective-permute-start | bytes 1523720 | tf_op jit(solution)/shard_map/ppermute | solution.py:533
  41.7 0.0 copy-done.5
  41.7 1.9 %collective-permute-start.2 = (f32[15,64,128]{2,1,0:T(8,128)S(1)}, f32[15,64,128]{2,1,0:T(8,128)S(1)}, u32[]{:S(2)}, u32[]{:S(2)}) collective-permute-start(f32[15,64,128]{2,1,0:T(8,128)S(1)} %copy-done.5), channel_id=1, source_target_pairs={{0,1},{1,0},{2,3},{3,2},{4,5},{5,4},{6,7},{7,6},{8,9},{9,8},{10,11... | collective-permute-start | bytes 1474568 | tf_op jit(solution)/shard_map/ppermute | solution.py:534
  44.3 1.2 %collective-permute-done.2.share_ref = f32[15,64,128]{2,1,0:T(8,128)S(1)} collective-permute-done((f32[15,64,128]{2,1,0:T(8,128)S(1)}, f32[15,64,128]{2,1,0:T(8,128)S(1)}, u32[]{:S(2)}, u32[]{:S(2)}) %collective-permute-start.2) | collective-permute-done | bytes 491552 | tf_op jit(solution)/shard_map/ppermute | solution.py:534
  45.5 0.0 collective-permute-done.1.swapped_hbm
  45.5 0.0 copy-done.1
  45.5 0.0 copy-done.4
  45.5 0.0 copy-start.2
  45.5 3.5 %field.1 = (bf16[8,128,128]{2,1,0:T(8,128)(2,1)}, f32[16,32,32]{2,1,0:T(8,128)S(1)}) custom-call(s32[2,31]{1,0:T(2,128)S(1)} %bitcast.7, s32[16,128]{1,0:T(8,128)S(1)} %get-tuple-element.14.other_hbm.owner_hbm, bf16[31,32,256]{2,1,0:T(8,128)(2,1)} %get-tuple-element.15.mine_hbm, bf16[31,32,256]{2,1,0:T(8,128)(2,1)} %collective-permute-done.received_hbm, ...), custom_call_target="tpu_custom_call" | custom-call | tf_op jit(solution)/shard_map/field/pallas_call | solution.py:537
  49.0 0.0 copy-done.3
  49.0 2.6 %all-to-all-done.1.tops_hbm = bf16[64,16,128]{2,1,0:T(8,128)(2,1)} async-done(((bf16[64,16,128]{2,1,0:T(8,128)(2,1)}), bf16[64,16,128]{2,1,0:T(8,128)(2,1)}, u32[]{:S(2)}, u32[]{:S(2)}) %all-to-all-start.1) | async-done | bytes 262176 | tf_op jit(solution)/shard_map/all_to_all | solution.py:536
  51.6 6.9 %all-to-all-start = ((bf16[8,128,128]{2,1,0:T(8,128)(2,1)}), bf16[8,128,128]{2,1,0:T(8,128)(2,1)S(1)}, u32[]{:S(2)}, u32[]{:S(2)}) async-start(bf16[8,128,128]{2,1,0:T(8,128)(2,1)} %get-tuple-element.17), calls=%async_computation | async-start | bytes 524288 | tf_op jit(solution)/shard_map/all_to_all | solution.py:575
  58.5 2.1 %top.1.extra_ref = f32[8,32,128]{2,1,0:T(8,128)S(1)} custom-call(s32[16,128]{1,0:T(8,128)} %copy-done.3, bf16[64,16,128]{2,1,0:T(8,128)(2,1)} %all-to-all-done.1.tops_hbm, bf16[8,64,128]{2,1,0:T(8,128)(2,1)} %get-tuple-element.19.matrix_hbm, f32[30,64,64]{2,1,0:T(8,128)S(1)} %copy-done), custom_call_target="tpu_custom_call" | custom-call | tf_op jit(solution)/shard_map/top/pallas_call | solution.py:576
  60.6 4.4 %all-to-all-done.parts_ref = bf16[8,128,128]{2,1,0:T(8,128)(2,1)S(1)} async-done(((bf16[8,128,128]{2,1,0:T(8,128)(2,1)}), bf16[8,128,128]{2,1,0:T(8,128)(2,1)S(1)}, u32[]{:S(2)}, u32[]{:S(2)}) %all-to-all-start) | async-done | bytes 262176 | tf_op jit(solution)/shard_map/all_to_all | solution.py:575
  65.0 0.0 copy-done.2
  65.0 1.0 %far.1 = f32[16,32,32]{2,1,0:T(8,128)} custom-call(bf16[8,128,128]{2,1,0:T(8,128)(2,1)S(1)} %all-to-all-done.parts_ref, f32[8,32,128]{2,1,0:T(8,128)S(1)} %top.1.extra_ref, bf16[16,32,64]{2,1,0:T(8,128)(2,1)S(1)} %bitcast.5, f32[16,32,32]{2,1,0:T(8,128)S(1)} %get-tuple-element.20.near_ref), custom_call_target="tpu_custom_call" | custom-call | tf_op jit(solution)/shard_map/far/pallas_call | solution.py:589
Async XLA Ops:
  0.0 45.5 %copy-start.1 = (f32[31,2,64,64]{3,2,1,0:T(8,128)S(1)}, f32[31,2,64,64]{3,2,1,0:T(8,128)}, u32[]{:S(2)}) copy-start(f32[31,2,64,64]{3,2,1,0:T(8,128)} %coupling_ref.1) | copy-start | bytes 3047428
  0.0 45.5 %copy-start.4 = (s32[31,2]{0,1:T(2,128)S(1)}, s32[31,2]{0,1:T(2,128)}, u32[]{:S(2)}) copy-start(s32[31,2]{0,1:T(2,128)} %param.16) | copy-start | bytes 748
  0.0 23.3 %copy-start = (f32[30,64,64]{2,1,0:T(8,128)S(1)}, f32[30,64,64]{2,1,0:T(8,128)}, u32[]{:S(2)}) copy-start(f32[30,64,64]{2,1,0:T(8,128)} %transfer_ref.5) | copy-start | bytes 1474564
  2.6 39.1 %copy-start.5 = (f32[15,64,128]{2,1,0:T(8,128)S(1)}, f32[15,64,128]{2,1,0:T(8,128)}, u32[]{:S(2)}) copy-start(f32[15,64,128]{2,1,0:T(8,128)} %get-tuple-element.16) | copy-start | bytes 1474564
  25.3 23.8 %copy-start.3 = (s32[16,128]{1,0:T(8,128)}, s32[16,128]{1,0:T(8,128)S(1)}, u32[]{:S(2)}) copy-start(s32[16,128]{1,0:T(8,128)S(1)} %get-tuple-element.14.other_hbm.owner_hbm) | copy-start | bytes 24580
  25.3 13.7 %collective-permute-start = (bf16[31,32,256]{2,1,0:T(8,128)(2,1)}, bf16[31,32,256]{2,1,0:T(8,128)(2,1)}, u32[]{:S(2)}, u32[]{:S(2)}) collective-permute-start(bf16[31,32,256]{2,1,0:T(8,128)(2,1)} %get-tuple-element.15.mine_hbm), channel_id=1, source_target_pairs={{0,8},{2,10},{4,12},{6,14},{8,16},{9,1},{10,18},{11,3},{12,20},{13... | collective-permute-start | bytes 1523720 | tf_op jit(solution)/shard_map/ppermute | solution.py:532
  26.6 25.0 %all-to-all-start.1 = ((bf16[64,16,128]{2,1,0:T(8,128)(2,1)}), bf16[64,16,128]{2,1,0:T(8,128)(2,1)}, u32[]{:S(2)}, u32[]{:S(2)}) async-start(bf16[64,16,128]{2,1,0:T(8,128)(2,1)} %get-tuple-element.18), calls=%async_computation.1 | async-start | bytes 524288 | tf_op jit(solution)/shard_map/all_to_all | solution.py:536
  38.9 6.5 %collective-permute-start.1 = (bf16[31,32,256]{2,1,0:T(8,128)(2,1)}, bf16[31,32,256]{2,1,0:T(8,128)(2,1)S(1)}, u32[]{:S(2)}, u32[]{:S(2)}) collective-permute-start(bf16[31,32,256]{2,1,0:T(8,128)(2,1)} %collective-permute-done.received_hbm), channel_id=1, source_target_pairs={{0,1},{1,0},{2,3},{3,2},{4,5},{5,4},{6,7},{7,6},{8,9},{9,8},{10,11... | collective-permute-start | bytes 1523720 | tf_op jit(solution)/shard_map/ppermute | solution.py:533
  41.7 3.8 %collective-permute-start.2 = (f32[15,64,128]{2,1,0:T(8,128)S(1)}, f32[15,64,128]{2,1,0:T(8,128)S(1)}, u32[]{:S(2)}, u32[]{:S(2)}) collective-permute-start(f32[15,64,128]{2,1,0:T(8,128)S(1)} %copy-done.5), channel_id=1, source_target_pairs={{0,1},{1,0},{2,3},{3,2},{4,5},{5,4},{6,7},{7,6},{8,9},{9,8},{10,11... | collective-permute-start | bytes 1474568 | tf_op jit(solution)/shard_map/ppermute | solution.py:534
  45.5 19.5 %copy-start.2 = (bf16[16,64,32]{1,2,0:T(8,128)(2,1)S(1)}, bf16[16,64,32]{1,2,0:T(8,128)(2,1)}, u32[]{:S(2)}) copy-start(bf16[16,64,32]{1,2,0:T(8,128)(2,1)} %param.13) | copy-start | bytes 196612
  51.6 13.4 %all-to-all-start = ((bf16[8,128,128]{2,1,0:T(8,128)(2,1)}), bf16[8,128,128]{2,1,0:T(8,128)(2,1)S(1)}, u32[]{:S(2)}, u32[]{:S(2)}) async-start(bf16[8,128,128]{2,1,0:T(8,128)(2,1)} %get-tuple-element.17), calls=%async_computation | async-start | bytes 524288 | tf_op jit(solution)/shard_map/all_to_all | solution.py:575

commit v4 on v3

--- a/solution.py
+++ b/solution.py
@@ -105,16 +105,12 @@
     basis_hbm,
     coupling_hbm,
     out_hbm,
-    share_hbm,
     out_ref,
-    share_ref,
     sources_ref,
     basis_ref,
     coupling_ref,
-    half_ref,
     list_ref,
     in_sem,
-    half_sem,
     out_sem,
 ):
     copies = fetch(
@@ -125,13 +121,6 @@
             (list_hbm, list_ref),
         ),
         in_sem,
-    )
-    halves = fetch(
-        [
-            (coupling_hbm.at[pl.ds(source, count)], half_ref.at[pl.ds(place, count)])
-            for place, source, count in half_of(1 - lax.axis_index("slab") % 2)
-        ],
-        half_sem,
     )
     for copy in copies:
         copy.wait()
@@ -160,13 +149,24 @@
     out_ref[OWNER_ROW : OWNER_ROW + 16, :] = listed.astype(f32).astype(bf16)
     out = pltpu.make_async_copy(out_ref, out_hbm, out_sem.at[0])
     out.start()
+    out.wait()
+
+
+def share_kernel(coupling_hbm, received_hbm, share_hbm, share_ref, half_ref, half_sem, out_sem):
+    del received_hbm
+    halves = fetch(
+        [
+            (coupling_hbm.at[pl.ds(source, count)], half_ref.at[pl.ds(place, count)])
+            for place, source, count in half_of(1 - lax.axis_index("slab") % 2)
+        ],
+        half_sem,
+    )
     for copy in halves:
         copy.wait()
     for i in range(HALF):
         share_ref[i] = jnp.concatenate([half_ref[i, 0], half_ref[i, 1]], axis=1)
-    share = pltpu.make_async_copy(share_ref, share_hbm, out_sem.at[1])
+    share = pltpu.make_async_copy(share_ref, share_hbm, out_sem)
     share.start()
-    out.wait()
     share.wait()
 
 
@@ -481,23 +481,20 @@
             **params,
         )
 
-    packed, share = call(
+    (packed,) = call(
         pack_kernel,
         "pack",
-        [((PACKED, 128), bf16, HBM), ((HALF, RANK, 128), f32, HBM)],
+        [((PACKED, 128), bf16, HBM)],
         hbm(4),
-        hbm(2),
+        hbm(1),
         [
             pltpu.VMEM((PACKED, 128), bf16),
-            pltpu.VMEM((HALF, RANK, 128), f32),
             pltpu.VMEM(sources.shape, bf16),
             pltpu.VMEM((LEAVES, PART, RANK), bf16),
             pltpu.VMEM(coupling.shape[1:], f32),
-            pltpu.VMEM((HALF, *coupling.shape[1:]), f32),
             pltpu.SMEM(listed.shape, jnp.int32),
             dma((4,)),
-            dma((len(LEVELS),)),
-            dma((2,)),
+            dma((1,)),
         ],
     )(
         pin(listed, HBM),
@@ -531,6 +528,19 @@
                 moves.append((m * SLABS + s, to * SLABS + s))
     received = lax.ppermute(mine, ("z", "y", "slab"), moves)
     swapped = lax.ppermute(received, "slab", [(s, s ^ 1) for s in range(SLABS)])
+    (share,) = call(
+        share_kernel,
+        "share",
+        [((HALF, RANK, 128), f32, HBM)],
+        hbm(2),
+        hbm(1),
+        [
+            pltpu.VMEM((HALF, RANK, 128), f32),
+            pltpu.VMEM((HALF, *coupling.shape[1:]), f32),
+            dma((len(LEVELS),)),
+            dma,
+        ],
+    )(pin(coupling, HBM), pin(received, HBM))
     share = lax.ppermute(share, "slab", [(s, s ^ 1) for s in range(SLABS)])
     mine, received, swapped = pin(mine, HBM), pin(received, HBM), pin(swapped, pltpu.VMEM)
     tops = lax.all_to_all(top, ("z", "y"), 0, 0)

time: 66.4 us -> 65.7 us (0.989)
  waiting for transfers between devices: 8.14 us -> 5.97 us
  Pallas kernels: 11.1 us -> 12.6 us
    all_to_all x1, waiting for transfers between devices: 2.57 us -> 0.19 us  [shards(): tops = lax.all_to_all(top, ('z', 'y'), 0, 0)]
    pallas_call x1 -> x2, Pallas kernels: 2.54 us -> 4.05 us  [the longest x1 2.19 us: shards(): call(share_kernel, 'share', [((HALF, RANK, 128), f32, HBM)], hbm(2), hbm(...]
  transfers between devices with their start and end apart: 5 -> 5, of which waited for: 3 -> 3; matrix products, arithmetic and copies ran while one was open for 0% -> 0% of each run, Pallas kernels for 9% -> 12%
where the time goes in v4:
time: 65.7 us; the launch traced here: 65.3 us
  starting transfers between devices  25.2 us (38%)
  blocking collectives  20.7 us (32%)
  Pallas kernels  12.6 us (19%)
  waiting for transfers between devices  5.97 us (9%)
  between operations  0.77 us (1%)
    all_gather x1, blocking collectives, shards(): gathered = lax.all_gather(packed, 'slab')  20.7 us
    all_to_all x1, starting transfers between devices, shards(): tops = lax.all_to_all(top, ('z', 'y'), 0, 0)  12.3 us
    all_to_all x1, starting transfers between devices, shards(): parts = lax.all_to_all(leaf, 'slab', 0, 0)  6.87 us
    all_to_all x1, waiting for transfers between devices, shards(): parts = lax.all_to_all(leaf, 'slab', 0, 0)  4.38 us
    pallas_call x1, Pallas kernels, shards(): call(field_kernel, 'field', [((SLABS, LEAVES // 4 * RHS, 128), bf16, HBM)...  3.51 us
    ppermute x1, starting transfers between devices, shards(): swapped = lax.ppermute(received, 'slab', [(s, s ^ 1) for s in range(SLABS)])  2.75 us
    pallas_call x1, Pallas kernels, shards(): call(share_kernel, 'share', [((HALF, RANK, 128), f32, HBM)], hbm(2), hbm(...  2.19 us
    pallas_call x1, Pallas kernels, shards(): call(top_kernel, 'top', [((LEAVES // 2, RHS, 128), f32)], hbm(3) + vmem(1...  2.12 us
  transfers between devices with their start and end apart: 5, of which 3 were waited for; matrix products, arithmetic and copies ran while one was open for 0% of the time, Pallas kernels for 12%

profile of v4, /device:TPU:1, one launch (start us, length us, event | category | flops | bytes accessed | tf_op | source)
XLA Modules:
  0.0 65.3 jit_solution(12700108683643781818)
XLA Ops:
  0.0 0.0 copy-start.1
  0.0 1.9 %pack.1 = bf16[464,128]{1,0:T(8,128)(2,1)} custom-call(s32[2,31]{1,0:T(2,128)} %bitcast.6, bf16[16,32,32]{2,1,0:T(8,128)(2,1)} %sources_hbm.1, bf16[16,32,64]{2,1,0:T(8,128)(2,1)} %bitcast.8, f32[31,2,64,64]{3,2,1,0:T(8,128)} %coupling_ref.1), custom_call_target="tpu_custom_call" | custom-call | tf_op jit(solution)/shard_map/pack/pallas_call | solution.py:484
  1.9 0.0 copy-start
  1.9 0.0 copy-start.4
  1.9 20.7 %all-gather = bf16[3712,128]{1,0:T(8,128)(2,1)S(1)} all-gather(bf16[464,128]{1,0:T(8,128)(2,1)} %pack.1), channel_id=2, replica_groups=mesh['z'=8,'y'=8,'slab'=8] {'slab'}, dimensions={0}, use_global_device_ids=true | all-gather | bytes 1069056 | tf_op jit(solution)/shard_map/all_gather | solution.py:505
  22.6 0.0 copy-done.1
  22.6 2.0 %up.1 = (bf16[31,32,256]{2,1,0:T(8,128)(2,1)}, bf16[64,16,128]{2,1,0:T(8,128)(2,1)}, bf16[8,64,128]{2,1,0:T(8,128)(2,1)}, s32[16,128]{1,0:T(8,128)S(1)}) custom-call(bf16[8,464,128]{2,1,0:T(8,128)(2,1)S(1)} %bitcast.4, f32[30,64,64]{2,1,0:T(8,128)S(1)} %copy-done.1), custom_call_target="tpu_custom_call" | custom-call | tf_op jit(solution)/shard_map/up/pallas_call | solution.py:506
  24.6 0.0 copy-start.3
  24.6 1.3 %collective-permute-start = (bf16[31,32,256]{2,1,0:T(8,128)(2,1)}, bf16[31,32,256]{2,1,0:T(8,128)(2,1)}, u32[]{:S(2)}, u32[]{:S(2)}) collective-permute-start(bf16[31,32,256]{2,1,0:T(8,128)(2,1)} %get-tuple-element.12.mine_hbm), channel_id=1, source_target_pairs={{0,8},{2,10},{4,12},{6,14},{8,16},{9,1},{10,18},{11,3},{12,20},{13... | collective-permute-start | bytes 1523720 | tf_op jit(solution)/shard_map/ppermute | solution.py:529
  25.9 12.3 %all-to-all-start.1 = ((bf16[64,16,128]{2,1,0:T(8,128)(2,1)}), bf16[64,16,128]{2,1,0:T(8,128)(2,1)}, u32[]{:S(2)}, u32[]{:S(2)}) async-start(bf16[64,16,128]{2,1,0:T(8,128)(2,1)} %get-tuple-element.14), calls=%async_computation.1 | async-start | bytes 524288 | tf_op jit(solution)/shard_map/all_to_all | solution.py:546
  38.3 0.0 collective-permute-done.received_hbm
  38.3 2.7 %collective-permute-start.1 = (bf16[31,32,256]{2,1,0:T(8,128)(2,1)}, bf16[31,32,256]{2,1,0:T(8,128)(2,1)S(1)}, u32[]{:S(2)}, u32[]{:S(2)}) collective-permute-start(bf16[31,32,256]{2,1,0:T(8,128)(2,1)} %collective-permute-done.received_hbm), channel_id=1, source_target_pairs={{0,1},{1,0},{2,3},{3,2},{4,5},{5,4},{6,7},{7,6},{8,9},{9,8},{10,11... | collective-permute-start | bytes 1523720 | tf_op jit(solution)/shard_map/ppermute | solution.py:530
  41.0 2.2 %share.1 = f32[15,64,128]{2,1,0:T(8,128)} custom-call(f32[31,2,64,64]{3,2,1,0:T(8,128)} %coupling_ref.1, bf16[31,32,256]{2,1,0:T(8,128)(2,1)} %collective-permute-done.received_hbm), custom_call_target="tpu_custom_call" | custom-call | tf_op jit(solution)/shard_map/share/pallas_call | solution.py:531
  43.2 1.9 %collective-permute-start.2 = (f32[15,64,128]{2,1,0:T(8,128)}, f32[15,64,128]{2,1,0:T(8,128)S(1)}, u32[]{:S(2)}, u32[]{:S(2)}) collective-permute-start(f32[15,64,128]{2,1,0:T(8,128)} %share.1), channel_id=1, source_target_pairs={{0,1},{1,0},{2,3},{3,2},{4,5},{5,4},{6,7},{7,6},{8,9},{9,8},{10,11... | collective-permute-start | bytes 1474568 | tf_op jit(solution)/shard_map/ppermute | solution.py:544
  45.8 1.4 %collective-permute-done.2.share_ref = f32[15,64,128]{2,1,0:T(8,128)S(1)} collective-permute-done((f32[15,64,128]{2,1,0:T(8,128)}, f32[15,64,128]{2,1,0:T(8,128)S(1)}, u32[]{:S(2)}, u32[]{:S(2)}) %collective-permute-start.2) | collective-permute-done | bytes 491552 | tf_op jit(solution)/shard_map/ppermute | solution.py:544
  47.2 0.0 collective-permute-done.1.swapped_hbm
  47.2 0.0 copy-done
  47.2 0.0 copy-done.4
  47.2 0.0 copy-start.2
  47.2 3.5 %field.1 = (bf16[8,128,128]{2,1,0:T(8,128)(2,1)}, f32[16,32,32]{2,1,0:T(8,128)S(1)}) custom-call(s32[2,31]{1,0:T(2,128)S(1)} %bitcast.7, s32[16,128]{1,0:T(8,128)S(1)} %get-tuple-element.11.other_hbm.owner_hbm, bf16[31,32,256]{2,1,0:T(8,128)(2,1)} %get-tuple-element.12.mine_hbm, bf16[31,32,256]{2,1,0:T(8,128)(2,1)} %collective-permute-done.received_hbm, ...), custom_call_target="tpu_custom_call" | custom-call | tf_op jit(solution)/shard_map/field/pallas_call | solution.py:547
  50.7 0.0 copy-done.3
  50.7 0.2 all-to-all-done.1.tops_hbm
  50.9 6.9 %all-to-all-start = ((bf16[8,128,128]{2,1,0:T(8,128)(2,1)}), bf16[8,128,128]{2,1,0:T(8,128)(2,1)S(1)}, u32[]{:S(2)}, u32[]{:S(2)}) async-start(bf16[8,128,128]{2,1,0:T(8,128)(2,1)} %get-tuple-element.13), calls=%async_computation | async-start | bytes 524288 | tf_op jit(solution)/shard_map/all_to_all | solution.py:585
  57.8 2.1 %top.1.extra_ref = f32[8,32,128]{2,1,0:T(8,128)S(1)} custom-call(s32[16,128]{1,0:T(8,128)} %copy-done.3, bf16[64,16,128]{2,1,0:T(8,128)(2,1)} %all-to-all-done.1.tops_hbm, bf16[8,64,128]{2,1,0:T(8,128)(2,1)} %get-tuple-element.15.matrix_hbm, f32[30,64,64]{2,1,0:T(8,128)S(1)} %copy-done.1), custom_call_target="tpu_custom_call" | custom-call | tf_op jit(solution)/shard_map/top/pallas_call | solution.py:586
  59.9 4.4 %all-to-all-done.parts_ref = bf16[8,128,128]{2,1,0:T(8,128)(2,1)S(1)} async-done(((bf16[8,128,128]{2,1,0:T(8,128)(2,1)}), bf16[8,128,128]{2,1,0:T(8,128)(2,1)S(1)}, u32[]{:S(2)}, u32[]{:S(2)}) %all-to-all-start) | async-done | bytes 262176 | tf_op jit(solution)/shard_map/all_to_all | solution.py:585
  64.3 0.0 copy-done.2
  64.3 1.0 %far.1 = f32[16,32,32]{2,1,0:T(8,128)} custom-call(bf16[8,128,128]{2,1,0:T(8,128)(2,1)S(1)} %all-to-all-done.parts_ref, f32[8,32,128]{2,1,0:T(8,128)S(1)} %top.1.extra_ref, bf16[16,32,64]{2,1,0:T(8,128)(2,1)S(1)} %bitcast.5, f32[16,32,32]{2,1,0:T(8,128)S(1)} %get-tuple-element.16.near_ref), custom_call_target="tpu_custom_call" | custom-call | tf_op jit(solution)/shard_map/far/pallas_call | solution.py:599
Async XLA Ops:
  0.0 22.6 %copy-start.1 = (f32[30,64,64]{2,1,0:T(8,128)S(1)}, f32[30,64,64]{2,1,0:T(8,128)}, u32[]{:S(2)}) copy-start(f32[30,64,64]{2,1,0:T(8,128)} %transfer_ref.5) | copy-start | bytes 1474564
  1.9 45.3 %copy-start = (f32[31,2,64,64]{3,2,1,0:T(8,128)S(1)}, f32[31,2,64,64]{3,2,1,0:T(8,128)}, u32[]{:S(2)}) copy-start(f32[31,2,64,64]{3,2,1,0:T(8,128)} %coupling_ref.1) | copy-start | bytes 3047428
  1.9 45.3 %copy-start.4 = (s32[31,2]{0,1:T(2,128)S(1)}, s32[31,2]{0,1:T(2,128)}, u32[]{:S(2)}) copy-start(s32[31,2]{0,1:T(2,128)} %param.16) | copy-start | bytes 748
  24.6 26.1 %copy-start.3 = (s32[16,128]{1,0:T(8,128)}, s32[16,128]{1,0:T(8,128)S(1)}, u32[]{:S(2)}) copy-start(s32[16,128]{1,0:T(8,128)S(1)} %get-tuple-element.11.other_hbm.owner_hbm) | copy-start | bytes 24580
  24.6 13.6 %collective-permute-start = (bf16[31,32,256]{2,1,0:T(8,128)(2,1)}, bf16[31,32,256]{2,1,0:T(8,128)(2,1)}, u32[]{:S(2)}, u32[]{:S(2)}) collective-permute-start(bf16[31,32,256]{2,1,0:T(8,128)(2,1)} %get-tuple-element.12.mine_hbm), channel_id=1, source_target_pairs={{0,8},{2,10},{4,12},{6,14},{8,16},{9,1},{10,18},{11,3},{12,20},{13... | collective-permute-start | bytes 1523720 | tf_op jit(solution)/shard_map/ppermute | solution.py:529
  25.9 25.0 %all-to-all-start.1 = ((bf16[64,16,128]{2,1,0:T(8,128)(2,1)}), bf16[64,16,128]{2,1,0:T(8,128)(2,1)}, u32[]{:S(2)}, u32[]{:S(2)}) async-start(bf16[64,16,128]{2,1,0:T(8,128)(2,1)} %get-tuple-element.14), calls=%async_computation.1 | async-start | bytes 524288 | tf_op jit(solution)/shard_map/all_to_all | solution.py:546
  38.3 8.9 %collective-permute-start.1 = (bf16[31,32,256]{2,1,0:T(8,128)(2,1)}, bf16[31,32,256]{2,1,0:T(8,128)(2,1)S(1)}, u32[]{:S(2)}, u32[]{:S(2)}) collective-permute-start(bf16[31,32,256]{2,1,0:T(8,128)(2,1)} %collective-permute-done.received_hbm), channel_id=1, source_target_pairs={{0,1},{1,0},{2,3},{3,2},{4,5},{5,4},{6,7},{7,6},{8,9},{9,8},{10,11... | collective-permute-start | bytes 1523720 | tf_op jit(solution)/shard_map/ppermute | solution.py:530
  43.2 4.0 %collective-permute-start.2 = (f32[15,64,128]{2,1,0:T(8,128)}, f32[15,64,128]{2,1,0:T(8,128)S(1)}, u32[]{:S(2)}, u32[]{:S(2)}) collective-permute-start(f32[15,64,128]{2,1,0:T(8,128)} %share.1), channel_id=1, source_target_pairs={{0,1},{1,0},{2,3},{3,2},{4,5},{5,4},{6,7},{7,6},{8,9},{9,8},{10,11... | collective-permute-start | bytes 1474568 | tf_op jit(solution)/shard_map/ppermute | solution.py:544
  47.2 17.1 %copy-start.2 = (bf16[16,64,32]{1,2,0:T(8,128)(2,1)S(1)}, bf16[16,64,32]{1,2,0:T(8,128)(2,1)}, u32[]{:S(2)}) copy-start(bf16[16,64,32]{1,2,0:T(8,128)(2,1)} %param.13) | copy-start | bytes 196612
  50.9 13.4 %all-to-all-start = ((bf16[8,128,128]{2,1,0:T(8,128)(2,1)}), bf16[8,128,128]{2,1,0:T(8,128)(2,1)S(1)}, u32[]{:S(2)}, u32[]{:S(2)}) async-start(bf16[8,128,128]{2,1,0:T(8,128)(2,1)} %get-tuple-element.13), calls=%async_computation | async-start | bytes 524288 | tf_op jit(solution)/shard_map/all_to_all | solution.py:585
